TPU v7x, 128 devices: a whole 4x4x4 slice. The times are simulated.
128 devices in a mesh: blk: 8 (over y, z_lo), head: 16 (over x, z_hi, core).
Axes of the slice: x: 4, y: 4, z: 4 (z_hi: 2, z_lo: 2; z = z_hi * 2 + z_lo), core: 2. Of those that a mesh axis runs over, the one named last changes fastest.
Arguments:
- queries: bfloat16 [20480, 2048], P(('blk', 'head')), may hold values from -64 to 64
- key_rows: bfloat16 [20480, 2048], P(('blk', 'head')), may hold values from -12 to 12
- value_rows: bfloat16 [20480, 2048], P(('blk', 'head')), may hold values from -6 to 6
- w_out: bfloat16 [2048, 3072], replicated, may hold values from -0.125 to 0.125
- shift_vec: float32 [3072], replicated, may hold values from -3 to 3
- scale_vec: float32 [3072], replicated, may hold values from -3 to 3
- w_final: bfloat16 [3072, 64], replicated, may hold values from -0.109375 to 0.109375
- w_conv: bfloat16 [3, 3, 3, 16, 512], replicated, may hold values from -0.3125 to 0.3125
Outputs:
- decoded: bfloat16 [8, 64, 160, 512], P('blk', None, 'head')
All inputs are finite; a program needn't handle non-finite values.
Results may differ from a plain program's by a relative error of at most 0.017.
Values may be sent and summed in bfloat16 or wider, within the bound.
No kernel may reach another device: no remote copies, remote signals or barrier semaphores. Data moves between devices by JAX's collectives and lax.ppermute only.
A program may use at most 448 MiB of HBM per device.

v0:
```python
import functools

import jax
import jax.numpy as jnp
import numpy as np
from jax import lax
from jax.experimental import pallas as pl
from jax.experimental.pallas import tpu as pltpu
from jax.sharding import Mesh, PartitionSpec as P

HD = 128
HEADS = 16
D = 3072
C_LAT = 16
C_VAE = 512
PW = 80
PH = 32
BANDS = 16
BAND = 5
WIDE = 8
AXES = ("y", "zl", "x", "zh", "c")
SIZES = (4, 2, 4, 2, 2)
PLANE = ("zl", "x", "zh")
SCALE_LOG2 = HD ** -0.5 * 1.4426950408889634
LIMIT = 1e30
NT = (((1,), (1,)), ((), ()))
STATE = HD + 16
MIB = 2 ** 20
ATTEND_MIB = 36


def dot_nt(a, b):
    return lax.dot_general(a, b, NT, preferred_element_type=jnp.float32)


def attention_kernel(*refs, pieces, first, filled):
    q_ref = refs[0]
    kv_refs = refs[1 : 1 + pieces]
    rest = refs[1 + pieces :]
    if filled:
        rest = rest[1:]
    if first:
        out_ref, keys_ref, vt_ref = rest
    else:
        in_ref, out_ref, keys_ref, vt_ref = rest
    starts = [0]
    for kv in kv_refs:
        starts.append(starts[-1] + kv.shape[0])

    @pl.when(pl.program_id(0) == 0)
    def _():
        for n, kv in enumerate(kv_refs):
            keys_ref[starts[n] : starts[n + 1], :] = kv[:, :HD]
            vt_ref[:, starts[n] : starts[n + 1]] = kv[:, HD:].T

    q_scaled = q_ref[...].astype(jnp.float32) * SCALE_LOG2
    q_hi = q_scaled.astype(jnp.bfloat16)
    q_lo = (q_scaled - q_hi.astype(jnp.float32)).astype(jnp.bfloat16)
    q_pair = jnp.concatenate([q_hi, q_lo], axis=1)
    cols = q_pair.shape[0]

    def scores_of(keys):
        return dot_nt(jnp.concatenate([keys, keys], axis=1), q_pair)

    if first:
        reference = jnp.max(scores_of(kv_refs[0][0:256, :HD]), axis=0, keepdims=True)
        total = jnp.zeros((8, cols), jnp.float32)
        acc = jnp.zeros((HD, cols), jnp.float32)
    else:
        reference = in_ref[HD + 8 : HD + 9, :]
        total = in_ref[HD : HD + 8, :]
        acc = in_ref[0:HD, :]
    for n, kv in enumerate(kv_refs):
        size = kv.shape[0]
        step = min(size, 1280)
        for at in range(0, size, step):
            weights = jnp.exp2(scores_of(kv[at : at + step, :HD]) - reference)
            total = total + jnp.sum(weights.reshape(step // 8, 8, cols), axis=0)
            acc = acc + jnp.dot(
                vt_ref[:, starts[n] + at : starts[n] + at + step],
                weights.astype(jnp.bfloat16),
                preferred_element_type=jnp.float32,
            )
    out_ref[0:HD, :] = acc
    out_ref[HD : HD + 8, :] = total
    out_ref[HD + 8 :, :] = jnp.broadcast_to(reference, (8, cols))
    safe = jnp.max(total) < LIMIT

    @pl.when(jnp.logical_not(safe))
    def _():
        if first:
            out_ref[0 : HD + 8, :] = jnp.zeros((HD + 8, cols), jnp.float32)
        else:
            out_ref[...] = in_ref[...]

        def absorb(i, carry):
            at = pl.multiple_of(i * 128, 128)
            scores = scores_of(keys_ref[pl.ds(at, 128), :])
            old = out_ref[HD + 8 : HD + 9, :]
            new = jnp.maximum(old, jnp.max(scores, axis=0, keepdims=True))
            rescale = jnp.exp2(old - new)
            weights = jnp.exp2(scores - new)
            out_ref[HD : HD + 8, :] = out_ref[HD : HD + 8, :] * rescale + jnp.sum(
                weights.reshape(16, 8, cols), axis=0
            )
            out_ref[0:HD, :] = out_ref[0:HD, :] * rescale + jnp.dot(
                vt_ref[:, pl.ds(at, 128)], weights.astype(jnp.bfloat16), preferred_element_type=jnp.float32
            )
            out_ref[HD + 8 :, :] = jnp.broadcast_to(new, (8, cols))
            return carry

        lax.fori_loop(0, starts[-1] // 128, absorb, 0)


def attend(q, kvs, state=None, columns=None, offset=0, fill=None, block=1280):
    rows = q.shape[0]
    first = state is None
    keys = sum(kv.shape[0] for kv in kvs)
    shift = offset // block
    write = shift if columns else 0
    in_specs = [pl.BlockSpec((block, HD), lambda i: (i, 0))]
    in_specs += [pl.BlockSpec(kv.shape, lambda i: (0, 0)) for kv in kvs]
    args = [q] + list(kvs)
    aliases = {}
    if not first:
        in_specs.append(pl.BlockSpec((STATE, block), lambda i: (0, i + shift)))
        args.append(state)
    if fill is not None:
        aliases = {len(args): 0}
        in_specs.append(pl.BlockSpec(memory_space=pl.ANY))
        args.append(fill)
    return pl.pallas_call(
        functools.partial(attention_kernel, pieces=len(kvs), first=first, filled=fill is not None),
        grid=(rows // block,),
        in_specs=in_specs,
        out_specs=pl.BlockSpec((STATE, block), lambda i: (0, i + write)),
        out_shape=jax.ShapeDtypeStruct((STATE, columns or rows), jnp.float32),
        scratch_shapes=[pltpu.VMEM((keys, HD), jnp.bfloat16), pltpu.VMEM((HD, keys), jnp.bfloat16)],
        input_output_aliases=aliases,
        compiler_params=pltpu.CompilerParams(vmem_limit_bytes=ATTEND_MIB * MIB),
        cost_estimate=pl.CostEstimate(
            flops=rows * keys * 6 * HD,
            bytes_accessed=rows * 1408 + keys * 512,
            transcendentals=rows * keys,
        ),
    )(*args)


def band_selection():
    chosen = np.zeros((BANDS, 8, WIDE, 8 * PW), np.float32)
    for band in range(BANDS):
        for col in range(WIDE):
            place = band * BAND - 1 + col
            if 0 <= place < PW:
                for row in range(8):
                    chosen[band, row, col, row * PW + place] = 1.0
    return chosen.reshape(BANDS * 8 * WIDE, 8 * PW)


def combine_kernel(mine_ref, other_ref, choose_ref, out_ref):
    lanes = 8 * PW
    for group in range(4):
        at = slice(group * lanes, (group + 1) * lanes)
        ref_a, ref_b = (mine_ref[HD + 8 : HD + 9, at], other_ref[HD + 8 : HD + 9, at])
        top = jnp.maximum(ref_a, ref_b)
        gain_a, gain_b = (jnp.exp2(ref_a - top), jnp.exp2(ref_b - top))
        total = jnp.sum(
            mine_ref[HD : HD + 8, at] * gain_a + other_ref[HD : HD + 8, at] * gain_b,
            axis=0,
            keepdims=True,
        )
        attended = (mine_ref[0:HD, at] * gain_a + other_ref[0:HD, at] * gain_b) / total
        banded = dot_nt(choose_ref[...], attended.astype(jnp.bfloat16)).astype(jnp.bfloat16)
        frame, half = divmod(group, 2)
        out_ref[frame * BANDS : (frame + 1) * BANDS, half * 64 : (half + 1) * 64, :] = banded.reshape(
            BANDS, 64, HD
        )


def combine(mine, other):
    choose = jnp.asarray(band_selection(), jnp.bfloat16)
    return pl.pallas_call(
        combine_kernel,
        out_shape=jax.ShapeDtypeStruct((2 * BANDS, 128, HD), jnp.bfloat16),
        compiler_params=pltpu.CompilerParams(vmem_limit_bytes=20 * MIB),
    )(mine, other, choose)


def window_selection():
    chosen = np.zeros((3, 4 * C_LAT, 2, 4, C_LAT), np.float32)
    for i in range(2):
        for col in range(4):
            side, j = divmod(col + 1, 2)
            for ch in range(C_LAT):
                chosen[side, 4 * ch + 2 * i + j, i, col, ch] = 1.0
    return chosen.reshape(3, 4 * C_LAT, 128)


TILE_N = 512


def project_kernel(
    band_ref, x_ref, w_ref, shift_ref, scale_ref, final_ref, choose_ref, out_ref, rows_ref, proj_ref, tiles_ref, sems
):
    tiles = D // TILE_N

    def fetch(n):
        return pltpu.make_async_copy(w_ref.at[:, pl.ds(n * TILE_N, TILE_N)], tiles_ref.at[n], sems.at[n])

    for n in range(tiles):
        fetch(n).start()
    for head in range(HEADS):
        for core in range(2):
            block = x_ref[head, core].reshape(8, 16, HD)
            for pair in range(8):
                at = pair * 32 + core * 16
                rows_ref[at : at + 16, head * HD : (head + 1) * HD] = block[pair]

    def multiply(n, total):
        fetch(n).wait()
        part = jnp.dot(rows_ref[...], tiles_ref[n], preferred_element_type=jnp.float32)
        proj_ref[n] = part
        return total + jnp.sum(part, axis=1, keepdims=True)

    total = jnp.zeros((PH * WIDE, 1), jnp.float32)
    for n in range(tiles):
        total = multiply(n, total)
    mean = total / D

    def measure(n, square):
        centered = proj_ref[n] - mean
        return square + jnp.sum(centered * centered, axis=1, keepdims=True)

    square = lax.fori_loop(0, tiles, measure, jnp.zeros((PH * WIDE, 1), jnp.float32), unroll=2)
    inverse = 1.0 / jnp.sqrt(square / D + 1e-06)

    def reduce(n, patches):
        at = pl.ds(pl.multiple_of(n * TILE_N, TILE_N), TILE_N)
        normed = (proj_ref[n] - mean) * inverse * (1.0 + scale_ref[:, at]) + shift_ref[:, at]
        return patches + jnp.dot(normed.astype(jnp.bfloat16), final_ref[at, :], preferred_element_type=jnp.float32)

    patches = lax.fori_loop(0, tiles, reduce, jnp.zeros((PH * WIDE, 4 * C_LAT), jnp.float32), unroll=2)
    patches = patches.astype(jnp.bfloat16).astype(jnp.float32)
    place = lax.rem(lax.broadcasted_iota(jnp.int32, patches.shape, 0), WIDE) + (band_ref[0] * BAND - 1)
    patches = jnp.where((place >= 0) & (place < PW), patches, 0.0)
    wide = jnp.zeros((PH * WIDE, 128), jnp.float32)
    for side in range(3):
        moved = patches if side == 0 else pltpu.roll(patches, PH * WIDE - side, 0)
        wide = wide + jnp.dot(moved.astype(jnp.bfloat16), choose_ref[side], preferred_element_type=jnp.float32)
    out_ref[...] = wide.astype(jnp.bfloat16)


def project(band, gathered, w_out, shift_vec, scale_vec, w_final):
    choose = jnp.asarray(window_selection(), jnp.bfloat16)
    vmem = pl.BlockSpec(memory_space=pltpu.VMEM)
    return pl.pallas_call(
        project_kernel,
        in_specs=[pl.BlockSpec(memory_space=pltpu.SMEM), vmem, pl.BlockSpec(memory_space=pl.ANY)] + [vmem] * 4,
        out_specs=vmem,
        out_shape=jax.ShapeDtypeStruct((PH * WIDE, 128), jnp.bfloat16),
        scratch_shapes=[
            pltpu.VMEM((PH * WIDE, HEADS * HD), jnp.bfloat16),
            pltpu.VMEM((D // TILE_N, PH * WIDE, TILE_N), jnp.float32),
            pltpu.VMEM((D // TILE_N, HEADS * HD, TILE_N), jnp.bfloat16),
            pltpu.SemaphoreType.DMA((D // TILE_N,)),
        ],
        compiler_params=pltpu.CompilerParams(vmem_limit_bytes=52 * MIB),
    )(band, gathered, w_out, shift_vec.reshape(1, D), scale_vec.reshape(1, D), w_final, choose)


def conv_kernel(frame_ref, now_ref, one_ref, two_ref, w_ref, out_ref, taps_ref, grid_ref, spread_ref):
    rows = PH * WIDE
    taps_ref[...] = jnp.zeros_like(taps_ref)
    for odd in range(2):
        for a in range(3):
            for b in range(3):
                y = odd + b - 1
                offset = {-1: 192, 0: 0, 1: 64, 2: 128}[y]
                for j in range(2):
                    for e in range(3):
                        at = offset + (j + e) * C_LAT
                        tap = ((a * 3 + b) * 3 + e) * C_LAT
                        taps_ref[odd, a, at : at + C_LAT, j * C_VAE : (j + 1) * C_VAE] = w_ref[tap : tap + C_LAT, :]
    frame = frame_ref[0]
    now = now_ref[...].astype(jnp.float32)
    one = jnp.where(frame >= 1, one_ref[...].astype(jnp.float32), now)
    two = jnp.where(frame >= 2, two_ref[...].astype(jnp.float32), one)
    gap = jnp.zeros((WIDE, 128), jnp.float32)
    for a, grid in enumerate((two, one, now)):
        grid_ref[a, 0:WIDE, :] = gap
        grid_ref[a, WIDE : WIDE + rows, :] = grid
        grid_ref[a, WIDE + rows :, :] = gap

    def column_major(a, down):
        parts = [grid_ref[a, pl.ds((1 + down) * WIDE + col, PH, stride=WIDE), :] for col in range(BAND)]
        return jnp.concatenate(parts, axis=0).astype(jnp.bfloat16)

    for odd in range(2):
        result = jnp.zeros((BAND * PH, 2 * C_VAE), jnp.float32)
        for a in range(3):
            window = jnp.concatenate([column_major(a, 0), column_major(a, 2 * odd - 1)], axis=1)
            result = result + jnp.dot(window, taps_ref[odd, a], preferred_element_type=jnp.float32)
        for col in range(BAND):
            for j in range(2):
                for part in range(C_VAE // 128):
                    at = j * C_VAE + part * 128
                    spread_ref[part, pl.ds((2 * col + j) * 2 * PH + odd, PH, stride=2), :] = result[
                        col * PH : (col + 1) * PH, at : at + 128
                    ]
    for part in range(C_VAE // 128):
        final = spread_ref[part].reshape(2 * BAND, 2 * PH, 128)
        out_ref[:, :, part * 128 : (part + 1) * 128] = final.astype(jnp.bfloat16)


def convolve(frame, now, one, two, w_conv):
    return pl.pallas_call(
        conv_kernel,
        grid=(1,),
        in_specs=[pl.BlockSpec(memory_space=pltpu.SMEM)]
        + [pl.BlockSpec((PH * WIDE, 128), lambda i: (0, 0))] * 3
        + [pl.BlockSpec((27 * C_LAT, C_VAE), lambda i: (0, 0))],
        out_specs=pl.BlockSpec((2 * BAND, 2 * PH, C_VAE), lambda i: (0, 0, 0)),
        out_shape=jax.ShapeDtypeStruct((2 * BAND, 2 * PH, C_VAE), jnp.bfloat16),
        scratch_shapes=[
            pltpu.VMEM((2, 3, 256, 2 * C_VAE), jnp.bfloat16),
            pltpu.VMEM((3, (PH + 2) * WIDE, 128), jnp.float32),
            pltpu.VMEM((C_VAE // 128, 4 * BAND * PH, 128), jnp.float32),
        ],
        compiler_params=pltpu.CompilerParams(vmem_limit_bytes=24 * MIB),
    )(frame, now, one, two, w_conv.reshape(27 * C_LAT, C_VAE))


def ring(x, axis, by):
    count = lax.axis_size(axis)
    return lax.ppermute(x, axis, [(i, (i + by) % count) for i in range(count)])


def later(x, by):
    count = lax.axis_size(("y", "zl"))
    return lax.ppermute(x, ("y", "zl"), [(i, i + by) for i in range(count - by)])


def per_device(queries, key_rows, value_rows, w_out, shift_vec, scale_vec, w_final, w_conv):
    tokens = queries.shape[0]

    def by_head(x):
        return x.reshape(tokens, HEADS, HD).transpose(1, 0, 2)

    outgoing = jnp.concatenate([by_head(key_rows), by_head(value_rows), by_head(queries)], axis=2)
    incoming = lax.all_to_all(outgoing, PLANE, 0, 0, tiled=True).reshape(HEADS * tokens, 3 * HD)
    half = HEADS * tokens // 2
    kv = incoming[:, : 2 * HD]
    kv_a, kv_b = (kv[:half], kv[half:])
    q_mine = incoming[:, 2 * HD :]
    below_a, above_b = (ring(kv_a, "y", 1), ring(kv_b, "y", -1))
    q_theirs = ring(q_mine, "c", 1)
    columns = 4 * half
    state = attend(q_mine, [kv_a, kv_b], columns=columns)
    kv_a, kv_b, q_theirs, state = lax.optimization_barrier((kv_a, kv_b, q_theirs, state))
    below_b, above_a = (ring(kv_b, "y", 1), ring(kv_a, "y", -1))
    state = attend(q_theirs, [kv_a, kv_b], columns=columns, offset=2 * half, fill=state)
    q_all = jnp.concatenate([q_mine, q_theirs], axis=0)
    below_a, above_b, state = lax.optimization_barrier((below_a, above_b, state))
    far_a, far_b = (ring(below_a, "y", 1), ring(above_b, "y", -1))
    state = attend(q_all, [below_a, above_b], state)
    below_b, above_a, state = lax.optimization_barrier((below_b, above_a, state))
    state = attend(q_all, [below_b, above_a], state)
    far_a, far_b, state = lax.optimization_barrier((far_a, far_b, state))
    theirs = attend(q_theirs, [far_a, far_b], state, offset=2 * half)
    theirs = ring(theirs, "c", 1)
    mine = attend(q_mine, [far_a, far_b], state)
    banded = combine(mine, theirs)
    gathered = lax.all_to_all(banded, ("zl", "x", "zh", "c"), 0, 0, tiled=True)
    gathered = gathered.reshape(HEADS, 2, 128, HD)
    band = lax.axis_index(("x", "zh", "c")).astype(jnp.int32).reshape(1)
    frame = lax.axis_index(("y", "zl")).astype(jnp.int32).reshape(1)
    now = project(band, gathered, w_out, shift_vec, scale_vec, w_final)
    decoded = convolve(frame, now, later(now, 1), later(now, 2), w_conv)
    return decoded.transpose(1, 0, 2)[None]


def solution(mesh):
    fine = Mesh(mesh.devices.reshape(SIZES), AXES)
    rows = P(AXES, None)
    return jax.shard_map(
        per_device,
        mesh=fine,
        in_specs=(rows, rows, rows, P(), P(), P(), P(), P()),
        out_specs=P(("y", "zl"), None, ("x", "zh", "c"), None),
        check_vma=False,
    )
```

profile of v0, /device:TPU:40, one launch (start us, length us, event | category | flops | bytes accessed | tf_op | source)
XLA Modules:
  0.0 149.9 jit_solution(11546004705553962643)
XLA Ops:
  0.0 0.0 copy-start
  0.0 1.3 bitcast_bitcast_fusion.2
  1.3 0.0 copy-done
  1.3 1.3 bitcast_bitcast_fusion
  2.6 0.3 pad_maximum_fusion
  2.9 33.3 %all_to_all.10 = bf16[16,160,384]{2,1,0:T(8,128)(2,1)S(1)} all-to-all(bf16[16,160,384]{2,1,0:T(8,128)(2,1)S(1)} %pad_maximum_fusion), channel_id=1, replica_groups=mesh['y'=4,'zl'=2,'x'=4,'zh'=2,'c'=2] {'zl','x','zh'}, dimensions={0} | all-to-all | bytes 3932160 | tf_op jit(solution)/shard_map/all_to_all | solution.py:350
  36.2 0.1 collective-permute-start.2
  36.3 0.1 fusion
  36.4 1.6 %collective-permute-start = (bf16[1280,256]{1,0:T(8,128)(2,1)S(1)}, bf16[1280,256]{1,0:T(8,128)(2,1)S(1)}, u32[]{:S(2)}, u32[]{:S(2)}) collective-permute-start(bf16[1280,256]{1,0:T(8,128)(2,1)S(1)} %get-tuple-element.19.refs_1_), channel_id=1, source_target_pairs={{0,32},{32,64},{64,96},{96,0},{1,33},{33,65},{65,97},{97,1},{2,34}... | collective-permute-start | bytes 1966088 | tf_op jit(solution)/shard_map/ppermute | solution.py:335
  38.0 0.5 collective-permute-start.1
  38.5 6.3 %shard_map.100.refs_3_ = f32[144,5120]{1,0:T(8,128)S(1)} custom-call(bf16[2560,128]{1,0:T(8,128)(2,1)S(1)} %slice.15.refs_0_, bf16[1280,256]{1,0:T(8,128)(2,1)S(1)} %get-tuple-element.19.refs_1_, bf16[1280,256]{1,0:T(8,128)(2,1)S(1)} %get-tuple-element.20.refs_2_), custom_call_target="tpu_custom_call" | custom-call | flops 5033164800 | bytes 4915200 | tf_op jit(solution)/shard_map/pallas_call | solution.py:132
  44.8 0.0 collective-permute-done.2.refs_0_
  44.8 14.3 %collective-permute-start.5 = (bf16[1280,256]{1,0:T(8,128)(2,1)S(1)}, bf16[1280,256]{1,0:T(8,128)(2,1)S(1)}, u32[]{:S(2)}, u32[]{:S(2)}) collective-permute-start(bf16[1280,256]{1,0:T(8,128)(2,1)S(1)} %get-tuple-element.20.refs_2_), channel_id=1, source_target_pairs={{0,32},{32,64},{64,96},{96,0},{1,33},{33,65},{65,97},{97,1},{2,34}... | collective-permute-start | bytes 1966088 | tf_op jit(solution)/shard_map/ppermute | solution.py:335
  59.1 0.0 collective-permute-start.6
  59.1 6.3 %shard_map.101.refs_3_ = f32[144,5120]{1,0:T(8,128)S(1)} custom-call(bf16[2560,128]{1,0:T(8,128)(2,1)S(1)} %collective-permute-done.2.refs_0_, bf16[1280,256]{1,0:T(8,128)(2,1)S(1)} %get-tuple-element.19.refs_1_, bf16[1280,256]{1,0:T(8,128)(2,1)S(1)} %get-tuple-element.20.refs_2_, f32[144,5120]{1,0:T(8,128)S(1)} %shard_map.100.refs_3_), custom_call_target="tpu_custom_call", output_to_operand_aliasing={{}: (3, {})} | custom-call | flops 5033164800 | bytes 4915200 | tf_op jit(solution)/shard_map/pallas_call | solution.py:132
  65.4 0.1 pad_maximum_fusion.1.refs_0_
  65.5 0.0 collective-permute-done.refs_1_
  65.5 0.0 collective-permute-done.1.refs_2_
  65.5 2.1 %collective-permute-start.3 = (bf16[1280,256]{1,0:T(8,128)(2,1)S(1)}, bf16[1280,256]{1,0:T(8,128)(2,1)S(1)}, u32[]{:S(2)}, u32[]{:S(2)}) collective-permute-start(bf16[1280,256]{1,0:T(8,128)(2,1)S(1)} %collective-permute-done.refs_1_), channel_id=1, source_target_pairs={{0,32},{32,64},{64,96},{96,0},{1,33},{33,65},{65,97},{97,1},{2,34}... | collective-permute-start | bytes 1966088 | tf_op jit(solution)/shard_map/ppermute | solution.py:335
  67.6 0.2 collective-permute-start.4
  67.8 12.2 %shard_map.102.refs_3_ = f32[144,5120]{1,0:T(8,128)S(1)} custom-call(bf16[5120,128]{1,0:T(8,128)(2,1)S(1)} %pad_maximum_fusion.1.refs_0_, bf16[1280,256]{1,0:T(8,128)(2,1)S(1)} %collective-permute-done.refs_1_, bf16[1280,256]{1,0:T(8,128)(2,1)S(1)} %collective-permute-done.1.refs_2_, f32[144,5120]{1,0:T(8,128)S(1)} %shard_map.101.refs_3_), custom_call_target="tpu_custom_call" | custom-call | flops 10066329600 | bytes 8519680 | tf_op jit(solution)/shard_map/pallas_call | solution.py:132
  80.0 0.0 collective-permute-done.5.refs_1_
  80.0 0.0 collective-permute-done.6.refs_2_
  80.0 12.2 %shard_map.103.refs_3_ = f32[144,5120]{1,0:T(8,128)S(1)} custom-call(bf16[5120,128]{1,0:T(8,128)(2,1)S(1)} %pad_maximum_fusion.1.refs_0_, bf16[1280,256]{1,0:T(8,128)(2,1)S(1)} %collective-permute-done.5.refs_1_, bf16[1280,256]{1,0:T(8,128)(2,1)S(1)} %collective-permute-done.6.refs_2_, f32[144,5120]{1,0:T(8,128)S(1)} %shard_map.102.refs_3_), custom_call_target="tpu_custom_call" | custom-call | flops 10066329600 | bytes 8519680 | tf_op jit(solution)/shard_map/pallas_call | solution.py:132
  92.2 0.0 collective-permute-done.3.refs_1_
  92.2 0.0 collective-permute-done.4.refs_2_
  92.2 6.3 %shard_map.105 = f32[144,2560]{1,0:T(8,128)S(1)} custom-call(bf16[2560,128]{1,0:T(8,128)(2,1)S(1)} %collective-permute-done.2.refs_0_, bf16[1280,256]{1,0:T(8,128)(2,1)S(1)} %collective-permute-done.3.refs_1_, bf16[1280,256]{1,0:T(8,128)(2,1)S(1)} %collective-permute-done.4.refs_2_, f32[144,5120]{1,0:T(8,128)S(1)} %shard_map.103.refs_3_), custom_call_target="tpu_custom_call" | custom-call | flops 5033164800 | bytes 4915200 | tf_op jit(solution)/shard_map/pallas_call | solution.py:132
  98.5 0.0 copy-start.1
  98.5 0.9 collective-permute-start.7
  99.4 6.2 %shard_map.104.mine_ref = f32[144,2560]{1,0:T(8,128)S(1)} custom-call(bf16[2560,128]{1,0:T(8,128)(2,1)S(1)} %slice.15.refs_0_, bf16[1280,256]{1,0:T(8,128)(2,1)S(1)} %collective-permute-done.3.refs_1_, bf16[1280,256]{1,0:T(8,128)(2,1)S(1)} %collective-permute-done.4.refs_2_, f32[144,5120]{1,0:T(8,128)S(1)} %shard_map.103.refs_3_), custom_call_target="tpu_custom_call" | custom-call | flops 5033164800 | bytes 4915200 | tf_op jit(solution)/shard_map/pallas_call | solution.py:132
  105.6 0.0 collective-permute-done.7.other_ref
  105.6 0.0 copy-done.1
  105.6 2.6 %shard_map.106 = bf16[32,128,128]{2,1,0:T(8,128)(2,1)} custom-call(f32[144,2560]{1,0:T(8,128)S(1)} %shard_map.104.mine_ref, f32[144,2560]{1,0:T(8,128)S(1)} %collective-permute-done.7.other_ref, bf16[1024,640]{1,0:T(8,128)(2,1)S(1)} %copy-done.1), custom_call_target="tpu_custom_call" | custom-call | tf_op jit(solution)/shard_map/pallas_call | solution.py:182
  108.2 5.3 %all-to-all-start.1 = ((bf16[32,128,128]{2,1,0:T(8,128)(2,1)}), bf16[32,128,128]{2,1,0:T(8,128)(2,1)S(1)}, u32[]{:S(2)}, u32[]{:S(2)}) async-start(bf16[32,128,128]{2,1,0:T(8,128)(2,1)} %shard_map.106), calls=%async_computation.1 | async-start | bytes 2097152 | tf_op jit(solution)/shard_map/all_to_all | solution.py:373
  113.5 0.0 copy-done.6
  113.5 0.4 copy.15.final_ref
  113.9 15.8 %all-to-all-done.1 = bf16[32,128,128]{2,1,0:T(8,128)(2,1)S(1)} async-done(((bf16[32,128,128]{2,1,0:T(8,128)(2,1)}), bf16[32,128,128]{2,1,0:T(8,128)(2,1)S(1)}, u32[]{:S(2)}, u32[]{:S(2)}) %all-to-all-start.1) | async-done | bytes 1048608 | tf_op jit(solution)/shard_map/all_to_all | solution.py:373
  129.7 0.0 copy-done.3
  129.7 0.0 copy-done.4
  129.7 0.0 copy-done.5
  129.7 0.0 copy-start.2
  129.7 8.4 %shard_map.107.now_ref = bf16[256,128]{1,0:T(8,128)(2,1)S(1)} custom-call(s32[1]{0:T(128)} %bitcast.1.band_ref, bf16[16,2,128,128]{3,2,1,0:T(8,128)(2,1)S(1)} %bitcast.31, bf16[2048,3072]{1,0:T(8,128)(2,1)} %w_ref.1, f32[1,3072]{1,0:T(1,128)S(1)} %bitcast.33, f32[1,3072]{1,0:T(1,128)S(1)} %bitcast.34, bf16[3072,64]{1,0:T(8,128)(2,1)S(1)} %copy.15.final_ref, ...), custom_call_target="tpu_custom_call" | custom-call | tf_op jit(solution)/shard_map/pallas_call | solution.py:256
  138.1 3.9 %collective-permute-start.8 = (bf16[256,128]{1,0:T(8,128)(2,1)S(1)}, bf16[256,128]{1,0:T(8,128)(2,1)S(1)}, u32[]{:S(2)}, u32[]{:S(2)}) collective-permute-start(bf16[256,128]{1,0:T(8,128)(2,1)S(1)} %shard_map.107.now_ref), channel_id=1, source_target_pairs={{0,16},{16,32},{32,48},{48,64},{64,80},{80,96},{96,112},{1,17},{17... | collective-permute-start | bytes 196616 | tf_op jit(solution)/shard_map/ppermute | solution.py:340
  142.1 3.2 %collective-permute-start.9 = (bf16[256,128]{1,0:T(8,128)(2,1)S(1)}, bf16[256,128]{1,0:T(8,128)(2,1)S(1)}, u32[]{:S(2)}, u32[]{:S(2)}) collective-permute-start(bf16[256,128]{1,0:T(8,128)(2,1)S(1)} %shard_map.107.now_ref), channel_id=1, source_target_pairs={{0,32},{16,48},{32,64},{48,80},{64,96},{80,112},{1,33},{17,49},{33... | collective-permute-start | bytes 196616 | tf_op jit(solution)/shard_map/ppermute | solution.py:340
  145.3 0.0 collective-permute-done.8.one_ref
  145.3 2.9 %collective-permute-done.9.two_ref = bf16[256,128]{1,0:T(8,128)(2,1)S(1)} collective-permute-done((bf16[256,128]{1,0:T(8,128)(2,1)S(1)}, bf16[256,128]{1,0:T(8,128)(2,1)S(1)}, u32[]{:S(2)}, u32[]{:S(2)}) %collective-permute-start.9) | collective-permute-done | bytes 65568 | tf_op jit(solution)/shard_map/ppermute | solution.py:340
  148.2 0.0 copy-done.2
  148.2 1.6 %shard_map.108 = bf16[10,64,512]{2,1,0:T(8,128)(2,1)} custom-call(s32[1]{0:T(128)} %bitcast.frame_ref, bf16[256,128]{1,0:T(8,128)(2,1)S(1)} %shard_map.107.now_ref, bf16[256,128]{1,0:T(8,128)(2,1)S(1)} %collective-permute-done.8.one_ref, bf16[256,128]{1,0:T(8,128)(2,1)S(1)} %collective-permute-done.9.two_ref, bf16[432,512]{1,0:T(8,128)(2,1)S(1)} %bitcast.32), custom_call_target="tpu_custom_call" | custom-call | tf_op jit(solution)/shard_map/pallas_call | solution.py:316
  (5 shorter events, 0.0 us)
Async XLA Ops:
  0.0 1.3 copy-start
  36.2 8.6 %collective-permute-start.2 = (bf16[2560,128]{1,0:T(8,128)(2,1)S(1)}, bf16[2560,128]{1,0:T(8,128)(2,1)S(1)}, u32[]{:S(2)}, u32[]{:S(2)}) collective-permute-start(bf16[2560,128]{1,0:T(8,128)(2,1)S(1)} %slice.15.refs_0_), channel_id=1, source_target_pairs={{0,1},{1,0},{2,3},{3,2},{4,5},{5,4},{6,7},{7,6},{8,9},{9,8},{10,11... | collective-permute-start | bytes 1966088 | tf_op jit(solution)/shard_map/ppermute | solution.py:335
  36.4 29.1 %collective-permute-start = (bf16[1280,256]{1,0:T(8,128)(2,1)S(1)}, bf16[1280,256]{1,0:T(8,128)(2,1)S(1)}, u32[]{:S(2)}, u32[]{:S(2)}) collective-permute-start(bf16[1280,256]{1,0:T(8,128)(2,1)S(1)} %get-tuple-element.19.refs_1_), channel_id=1, source_target_pairs={{0,32},{32,64},{64,96},{96,0},{1,33},{33,65},{65,97},{97,1},{2,34}... | collective-permute-start | bytes 1966088 | tf_op jit(solution)/shard_map/ppermute | solution.py:335
  38.0 27.4 %collective-permute-start.1 = (bf16[1280,256]{1,0:T(8,128)(2,1)S(1)}, bf16[1280,256]{1,0:T(8,128)(2,1)S(1)}, u32[]{:S(2)}, u32[]{:S(2)}) collective-permute-start(bf16[1280,256]{1,0:T(8,128)(2,1)S(1)} %get-tuple-element.20.refs_2_), channel_id=1, source_target_pairs={{0,96},{32,0},{64,32},{96,64},{1,97},{33,1},{65,33},{97,65},{2,98}... | collective-permute-start | bytes 1966088 | tf_op jit(solution)/shard_map/ppermute | solution.py:335
  44.8 35.2 %collective-permute-start.5 = (bf16[1280,256]{1,0:T(8,128)(2,1)S(1)}, bf16[1280,256]{1,0:T(8,128)(2,1)S(1)}, u32[]{:S(2)}, u32[]{:S(2)}) collective-permute-start(bf16[1280,256]{1,0:T(8,128)(2,1)S(1)} %get-tuple-element.20.refs_2_), channel_id=1, source_target_pairs={{0,32},{32,64},{64,96},{96,0},{1,33},{33,65},{65,97},{97,1},{2,34}... | collective-permute-start | bytes 1966088 | tf_op jit(solution)/shard_map/ppermute | solution.py:335
  59.1 20.9 %collective-permute-start.6 = (bf16[1280,256]{1,0:T(8,128)(2,1)S(1)}, bf16[1280,256]{1,0:T(8,128)(2,1)S(1)}, u32[]{:S(2)}, u32[]{:S(2)}) collective-permute-start(bf16[1280,256]{1,0:T(8,128)(2,1)S(1)} %get-tuple-element.19.refs_1_), channel_id=1, source_target_pairs={{0,96},{32,0},{64,32},{96,64},{1,97},{33,1},{65,33},{97,65},{2,98}... | collective-permute-start | bytes 1966088 | tf_op jit(solution)/shard_map/ppermute | solution.py:335
  65.5 26.7 %collective-permute-start.3 = (bf16[1280,256]{1,0:T(8,128)(2,1)S(1)}, bf16[1280,256]{1,0:T(8,128)(2,1)S(1)}, u32[]{:S(2)}, u32[]{:S(2)}) collective-permute-start(bf16[1280,256]{1,0:T(8,128)(2,1)S(1)} %collective-permute-done.refs_1_), channel_id=1, source_target_pairs={{0,32},{32,64},{64,96},{96,0},{1,33},{33,65},{65,97},{97,1},{2,34}... | collective-permute-start | bytes 1966088 | tf_op jit(solution)/shard_map/ppermute | solution.py:335
  67.6 24.6 %collective-permute-start.4 = (bf16[1280,256]{1,0:T(8,128)(2,1)S(1)}, bf16[1280,256]{1,0:T(8,128)(2,1)S(1)}, u32[]{:S(2)}, u32[]{:S(2)}) collective-permute-start(bf16[1280,256]{1,0:T(8,128)(2,1)S(1)} %collective-permute-done.1.refs_2_), channel_id=1, source_target_pairs={{0,96},{32,0},{64,32},{96,64},{1,97},{33,1},{65,33},{97,65},{2,98}... | collective-permute-start | bytes 1966088 | tf_op jit(solution)/shard_map/ppermute | solution.py:335
  98.5 7.1 %copy-start.1 = (bf16[1024,640]{1,0:T(8,128)(2,1)S(1)}, bf16[1024,640]{1,0:T(8,128)(2,1)}, u32[]{:S(2)}) copy-start(bf16[1024,640]{1,0:T(8,128)(2,1)} %constant.27.clone.choose_ref) | copy-start | bytes 3932164
  98.5 7.1 %collective-permute-start.7 = (f32[144,2560]{1,0:T(8,128)S(1)}, f32[144,2560]{1,0:T(8,128)S(1)}, u32[]{:S(2)}, u32[]{:S(2)}) collective-permute-start(f32[144,2560]{1,0:T(8,128)S(1)} %shard_map.105), channel_id=1, source_target_pairs={{0,1},{1,0},{2,3},{3,2},{4,5},{5,4},{6,7},{7,6},{8,9},{9,8},{10,11... | collective-permute-start | bytes 4423688 | tf_op jit(solution)/shard_map/ppermute | solution.py:335
  108.2 5.3 %copy-start.6 = (bf16[3072,64]{0,1:T(8,128)(2,1)S(1)}, bf16[3072,64]{0,1:T(8,128)(2,1)}, u32[]{:S(2)}) copy-start(bf16[3072,64]{0,1:T(8,128)(2,1)} %param.16) | copy-start | bytes 1179652
  108.2 21.5 %copy-start.3 = (bf16[3,64,128]{2,1,0:T(8,128)(2,1)S(1)}, bf16[3,64,128]{2,1,0:T(8,128)(2,1)}, u32[]{:S(2)}) copy-start(bf16[3,64,128]{2,1,0:T(8,128)(2,1)} %constant.28.clone.choose_ref) | copy-start | bytes 147460
  108.2 21.5 %copy-start.4 = (f32[3072]{0:T(1024)S(1)}, f32[3072]{0:T(1024)}, u32[]{:S(2)}) copy-start(f32[3072]{0:T(1024)} %param.14) | copy-start | bytes 36868
  108.2 21.5 %copy-start.5 = (f32[3072]{0:T(1024)S(1)}, f32[3072]{0:T(1024)}, u32[]{:S(2)}) copy-start(f32[3072]{0:T(1024)} %param.15) | copy-start | bytes 36868
  108.2 21.5 %all-to-all-start.1 = ((bf16[32,128,128]{2,1,0:T(8,128)(2,1)}), bf16[32,128,128]{2,1,0:T(8,128)(2,1)S(1)}, u32[]{:S(2)}, u32[]{:S(2)}) async-start(bf16[32,128,128]{2,1,0:T(8,128)(2,1)} %shard_map.106), calls=%async_computation.1 | async-start | bytes 2097152 | tf_op jit(solution)/shard_map/all_to_all | solution.py:373
  129.7 18.5 %copy-start.2 = (bf16[3,3,3,16,512]{4,3,2,1,0:T(8,128)(2,1)S(1)}, bf16[3,3,3,16,512]{4,3,2,1,0:T(8,128)(2,1)}, u32[]{:S(2)}) copy-start(bf16[3,3,3,16,512]{4,3,2,1,0:T(8,128)(2,1)} %param.17) | copy-start | bytes 1327108
  138.1 7.2 %collective-permute-start.8 = (bf16[256,128]{1,0:T(8,128)(2,1)S(1)}, bf16[256,128]{1,0:T(8,128)(2,1)S(1)}, u32[]{:S(2)}, u32[]{:S(2)}) collective-permute-start(bf16[256,128]{1,0:T(8,128)(2,1)S(1)} %shard_map.107.now_ref), channel_id=1, source_target_pairs={{0,16},{16,32},{32,48},{48,64},{64,80},{80,96},{96,112},{1,17},{17... | collective-permute-start | bytes 196616 | tf_op jit(solution)/shard_map/ppermute | solution.py:340
  142.1 6.2 %collective-permute-start.9 = (bf16[256,128]{1,0:T(8,128)(2,1)S(1)}, bf16[256,128]{1,0:T(8,128)(2,1)S(1)}, u32[]{:S(2)}, u32[]{:S(2)}) collective-permute-start(bf16[256,128]{1,0:T(8,128)(2,1)S(1)} %shard_map.107.now_ref), channel_id=1, source_target_pairs={{0,32},{16,48},{32,64},{48,80},{64,96},{80,112},{1,33},{17,49},{33... | collective-permute-start | bytes 196616 | tf_op jit(solution)/shard_map/ppermute | solution.py:340
where the time goes:
time: 150 us
  Pallas kernels  62 us (41%)
  blocking collectives  33.3 us (22%)
  starting transfers between devices  32 us (21%)
  waiting for transfers between devices  18.8 us (13%)
  local copies, waits for them, and re-layouts  3.12 us (2%)
    pallas_call x6, Pallas kernels, attend(): pl.pallas_call(functools.partial(attention_kernel, pieces=len(kvs), first...  49.5 us
    all_to_all x1, blocking collectives, per_device(): lax.all_to_all(outgoing, PLANE, 0, 0, tiled=True)  33.3 us
    ppermute x8, starting transfers between devices, ring(): return lax.ppermute(x, axis, [(i, (i + by) % count) for i in range(count)])  19.6 us
    all_to_all x1, waiting for transfers between devices, per_device(): gathered = lax.all_to_all(banded, ('zl', 'x', 'zh', 'c'), 0, 0, tiled=True)  15.8 us
    pallas_call x1, Pallas kernels, project(): pl.pallas_call(project_kernel, in_specs=[pl.BlockSpec(memory_space=pltpu....  8.37 us
    ppermute x2, starting transfers between devices, later(): lax.ppermute(x, ('y', 'zl'), [(i, i + by) for i in range(count - by)])  7.14 us
    all_to_all x1, starting transfers between devices, per_device(): gathered = lax.all_to_all(banded, ('zl', 'x', 'zh', 'c'), 0, 0, tiled=True)  5.28 us
  transfers between devices with their start and end apart: 11, of which 2 were waited for; matrix products, arithmetic and copies ran while one was open for 0% of the time, Pallas kernels for 29%

commit v1 on v0

--- a/solution.py
+++ b/solution.py
@@ -17,7 +17,8 @@
 PH = 32
 BANDS = 16
 BAND = 5
-WIDE = 8
+WIDE = 7
+ROWS = 8 * PW
 AXES = ("y", "zl", "x", "zh", "c")
 SIZES = (4, 2, 4, 2, 2)
 PLANE = ("zl", "x", "zh")
@@ -147,41 +148,42 @@
 
 
 def band_selection():
-    chosen = np.zeros((BANDS, 8, WIDE, 8 * PW), np.float32)
+    chosen = np.zeros((BANDS, WIDE, 8, ROWS), np.float32)
     for band in range(BANDS):
         for col in range(WIDE):
             place = band * BAND - 1 + col
             if 0 <= place < PW:
                 for row in range(8):
-                    chosen[band, row, col, row * PW + place] = 1.0
-    return chosen.reshape(BANDS * 8 * WIDE, 8 * PW)
+                    chosen[band, col, row, row * PW + place] = 1.0
+    return chosen.reshape(BANDS * WIDE * 8, ROWS)
 
 
 def combine_kernel(mine_ref, other_ref, choose_ref, out_ref):
-    lanes = 8 * PW
-    for group in range(4):
-        at = slice(group * lanes, (group + 1) * lanes)
-        ref_a, ref_b = (mine_ref[HD + 8 : HD + 9, at], other_ref[HD + 8 : HD + 9, at])
-        top = jnp.maximum(ref_a, ref_b)
-        gain_a, gain_b = (jnp.exp2(ref_a - top), jnp.exp2(ref_b - top))
-        total = jnp.sum(
-            mine_ref[HD : HD + 8, at] * gain_a + other_ref[HD : HD + 8, at] * gain_b,
-            axis=0,
-            keepdims=True,
-        )
-        attended = (mine_ref[0:HD, at] * gain_a + other_ref[0:HD, at] * gain_b) / total
-        banded = dot_nt(choose_ref[...], attended.astype(jnp.bfloat16)).astype(jnp.bfloat16)
-        frame, half = divmod(group, 2)
-        out_ref[frame * BANDS : (frame + 1) * BANDS, half * 64 : (half + 1) * 64, :] = banded.reshape(
-            BANDS, 64, HD
-        )
+    for frame in range(2):
+        halves = []
+        for half in range(2):
+            at = slice((2 * frame + half) * ROWS, (2 * frame + half + 1) * ROWS)
+            ref_a, ref_b = (mine_ref[HD + 8 : HD + 9, at], other_ref[HD + 8 : HD + 9, at])
+            top = jnp.maximum(ref_a, ref_b)
+            gain_a, gain_b = (jnp.exp2(ref_a - top), jnp.exp2(ref_b - top))
+            total = jnp.sum(
+                mine_ref[HD : HD + 8, at] * gain_a + other_ref[HD : HD + 8, at] * gain_b,
+                axis=0,
+                keepdims=True,
+            )
+            attended = (mine_ref[0:HD, at] * gain_a + other_ref[0:HD, at] * gain_b) / total
+            halves.append(attended.astype(jnp.bfloat16))
+        banded = dot_nt(choose_ref[...], jnp.concatenate(halves, axis=0))
+        upper, lower = (banded[:, n * HD : (n + 1) * HD].reshape(BANDS, WIDE, 8, HD) for n in range(2))
+        rows = jnp.concatenate([upper, lower], axis=2).astype(jnp.bfloat16)
+        out_ref[frame * BANDS : (frame + 1) * BANDS] = rows.reshape(BANDS, WIDE * 16, HD)
 
 
 def combine(mine, other):
     choose = jnp.asarray(band_selection(), jnp.bfloat16)
     return pl.pallas_call(
         combine_kernel,
-        out_shape=jax.ShapeDtypeStruct((2 * BANDS, 128, HD), jnp.bfloat16),
+        out_shape=jax.ShapeDtypeStruct((2 * BANDS, WIDE * 16, HD), jnp.bfloat16),
         compiler_params=pltpu.CompilerParams(vmem_limit_bytes=20 * MIB),
     )(mine, other, choose)
 
@@ -196,11 +198,20 @@
     return chosen.reshape(3, 4 * C_LAT, 128)
 
 
+def row_order():
+    chosen = np.zeros((BAND, PH, BAND, PH), np.float32)
+    for col in range(BAND):
+        for row in range(PH):
+            pair, core, low = (row // 4, row // 2 % 2, row % 2)
+            chosen[col, row, col, core * 16 + pair * 2 + low] = 1.0
+    return chosen.reshape(BAND * PH, BAND * PH)
+
+
 TILE_N = 512
 
 
 def project_kernel(
-    band_ref, x_ref, w_ref, shift_ref, scale_ref, final_ref, choose_ref, out_ref, rows_ref, proj_ref, tiles_ref, sems
+    band_ref, x_ref, w_ref, shift_ref, scale_ref, final_ref, choose_ref, order_ref, out_ref, rows_ref, proj_ref, tiles_ref, sems
 ):
     tiles = D // TILE_N
 
@@ -211,28 +222,23 @@
         fetch(n).start()
     for head in range(HEADS):
         for core in range(2):
-            block = x_ref[head, core].reshape(8, 16, HD)
-            for pair in range(8):
-                at = pair * 32 + core * 16
-                rows_ref[at : at + 16, head * HD : (head + 1) * HD] = block[pair]
-
-    def multiply(n, total):
+            for col in range(WIDE):
+                at = col * PH + core * 16
+                rows_ref[at : at + 16, head * HD : (head + 1) * HD] = x_ref[head, core, col * 16 : (col + 1) * 16, :]
+    total = 0.0
+    square = 0.0
+    for n in range(tiles):
         fetch(n).wait()
         part = jnp.dot(rows_ref[...], tiles_ref[n], preferred_element_type=jnp.float32)
         proj_ref[n] = part
-        return total + jnp.sum(part, axis=1, keepdims=True)
-
-    total = jnp.zeros((PH * WIDE, 1), jnp.float32)
-    for n in range(tiles):
-        total = multiply(n, total)
+        part_sum = jnp.sum(part, axis=1, keepdims=True)
+        if n == 0:
+            near = part_sum / TILE_N
+        total = total + part_sum
+        square = square + jnp.sum((part - near) * (part - near), axis=1, keepdims=True)
     mean = total / D
-
-    def measure(n, square):
-        centered = proj_ref[n] - mean
-        return square + jnp.sum(centered * centered, axis=1, keepdims=True)
-
-    square = lax.fori_loop(0, tiles, measure, jnp.zeros((PH * WIDE, 1), jnp.float32), unroll=2)
-    inverse = 1.0 / jnp.sqrt(square / D + 1e-06)
+    variance = square / D - (mean - near) * (mean - near)
+    inverse = 1.0 / jnp.sqrt(variance + 1e-06)
 
     def reduce(n, patches):
         at = pl.ds(pl.multiple_of(n * TILE_N, TILE_N), TILE_N)
@@ -240,24 +246,25 @@
         return patches + jnp.dot(normed.astype(jnp.bfloat16), final_ref[at, :], preferred_element_type=jnp.float32)
 
     patches = lax.fori_loop(0, tiles, reduce, jnp.zeros((PH * WIDE, 4 * C_LAT), jnp.float32), unroll=2)
-    patches = patches.astype(jnp.bfloat16).astype(jnp.float32)
-    place = lax.rem(lax.broadcasted_iota(jnp.int32, patches.shape, 0), WIDE) + (band_ref[0] * BAND - 1)
-    patches = jnp.where((place >= 0) & (place < PW), patches, 0.0)
-    wide = jnp.zeros((PH * WIDE, 128), jnp.float32)
+    place = lax.broadcasted_iota(jnp.int32, patches.shape, 0) // PH + (band_ref[0] * BAND - 1)
+    patches = jnp.where((place >= 0) & (place < PW), patches, 0.0).astype(jnp.bfloat16)
+    wide = 0.0
     for side in range(3):
-        moved = patches if side == 0 else pltpu.roll(patches, PH * WIDE - side, 0)
-        wide = wide + jnp.dot(moved.astype(jnp.bfloat16), choose_ref[side], preferred_element_type=jnp.float32)
+        moved = patches[side * PH : (side + BAND) * PH]
+        wide = wide + jnp.dot(moved, choose_ref[side], preferred_element_type=jnp.float32)
+    wide = jnp.dot(order_ref[...], wide.astype(jnp.bfloat16), preferred_element_type=jnp.float32)
     out_ref[...] = wide.astype(jnp.bfloat16)
 
 
 def project(band, gathered, w_out, shift_vec, scale_vec, w_final):
     choose = jnp.asarray(window_selection(), jnp.bfloat16)
+    order = jnp.asarray(row_order(), jnp.bfloat16)
     vmem = pl.BlockSpec(memory_space=pltpu.VMEM)
     return pl.pallas_call(
         project_kernel,
-        in_specs=[pl.BlockSpec(memory_space=pltpu.SMEM), vmem, pl.BlockSpec(memory_space=pl.ANY)] + [vmem] * 4,
+        in_specs=[pl.BlockSpec(memory_space=pltpu.SMEM), vmem, pl.BlockSpec(memory_space=pl.ANY)] + [vmem] * 5,
         out_specs=vmem,
-        out_shape=jax.ShapeDtypeStruct((PH * WIDE, 128), jnp.bfloat16),
+        out_shape=jax.ShapeDtypeStruct((BAND * PH, 128), jnp.bfloat16),
         scratch_shapes=[
             pltpu.VMEM((PH * WIDE, HEADS * HD), jnp.bfloat16),
             pltpu.VMEM((D // TILE_N, PH * WIDE, TILE_N), jnp.float32),
@@ -265,11 +272,11 @@
             pltpu.SemaphoreType.DMA((D // TILE_N,)),
         ],
         compiler_params=pltpu.CompilerParams(vmem_limit_bytes=52 * MIB),
-    )(band, gathered, w_out, shift_vec.reshape(1, D), scale_vec.reshape(1, D), w_final, choose)
-
-
-def conv_kernel(frame_ref, now_ref, one_ref, two_ref, w_ref, out_ref, taps_ref, grid_ref, spread_ref):
-    rows = PH * WIDE
+    )(band, gathered, w_out, shift_vec.reshape(1, D), scale_vec.reshape(1, D), w_final, choose, order)
+
+
+def conv_kernel(frame_ref, now_ref, one_ref, two_ref, w_ref, out_ref, taps_ref, spread_ref):
+    rows = BAND * PH
     taps_ref[...] = jnp.zeros_like(taps_ref)
     for odd in range(2):
         for a in range(3):
@@ -285,20 +292,15 @@
     now = now_ref[...].astype(jnp.float32)
     one = jnp.where(frame >= 1, one_ref[...].astype(jnp.float32), now)
     two = jnp.where(frame >= 2, two_ref[...].astype(jnp.float32), one)
-    gap = jnp.zeros((WIDE, 128), jnp.float32)
-    for a, grid in enumerate((two, one, now)):
-        grid_ref[a, 0:WIDE, :] = gap
-        grid_ref[a, WIDE : WIDE + rows, :] = grid
-        grid_ref[a, WIDE + rows :, :] = gap
-
-    def column_major(a, down):
-        parts = [grid_ref[a, pl.ds((1 + down) * WIDE + col, PH, stride=WIDE), :] for col in range(BAND)]
-        return jnp.concatenate(parts, axis=0).astype(jnp.bfloat16)
-
+    row = lax.rem(lax.broadcasted_iota(jnp.int32, (rows, 128), 0), PH)
     for odd in range(2):
-        result = jnp.zeros((BAND * PH, 2 * C_VAE), jnp.float32)
-        for a in range(3):
-            window = jnp.concatenate([column_major(a, 0), column_major(a, 2 * odd - 1)], axis=1)
+        result = jnp.zeros((rows, 2 * C_VAE), jnp.float32)
+        for a, grid in enumerate((two, one, now)):
+            if odd == 0:
+                beside = jnp.where(row == 0, 0.0, pltpu.roll(grid, 1, 0))
+            else:
+                beside = jnp.where(row == PH - 1, 0.0, pltpu.roll(grid, rows - 1, 0))
+            window = jnp.concatenate([grid, beside], axis=1).astype(jnp.bfloat16)
             result = result + jnp.dot(window, taps_ref[odd, a], preferred_element_type=jnp.float32)
         for col in range(BAND):
             for j in range(2):
@@ -317,13 +319,12 @@
         conv_kernel,
         grid=(1,),
         in_specs=[pl.BlockSpec(memory_space=pltpu.SMEM)]
-        + [pl.BlockSpec((PH * WIDE, 128), lambda i: (0, 0))] * 3
+        + [pl.BlockSpec((BAND * PH, 128), lambda i: (0, 0))] * 3
         + [pl.BlockSpec((27 * C_LAT, C_VAE), lambda i: (0, 0))],
         out_specs=pl.BlockSpec((2 * BAND, 2 * PH, C_VAE), lambda i: (0, 0, 0)),
         out_shape=jax.ShapeDtypeStruct((2 * BAND, 2 * PH, C_VAE), jnp.bfloat16),
         scratch_shapes=[
             pltpu.VMEM((2, 3, 256, 2 * C_VAE), jnp.bfloat16),
-            pltpu.VMEM((3, (PH + 2) * WIDE, 128), jnp.float32),
             pltpu.VMEM((C_VAE // 128, 4 * BAND * PH, 128), jnp.float32),
         ],
         compiler_params=pltpu.CompilerParams(vmem_limit_bytes=24 * MIB),
@@ -371,7 +372,7 @@
     mine = attend(q_mine, [far_a, far_b], state)
     banded = combine(mine, theirs)
     gathered = lax.all_to_all(banded, ("zl", "x", "zh", "c"), 0, 0, tiled=True)
-    gathered = gathered.reshape(HEADS, 2, 128, HD)
+    gathered = gathered.reshape(HEADS, 2, WIDE * 16, HD)
     band = lax.axis_index(("x", "zh", "c")).astype(jnp.int32).reshape(1)
     frame = lax.axis_index(("y", "zl")).astype(jnp.int32).reshape(1)
     now = project(band, gathered, w_out, shift_vec, scale_vec, w_final)

time: 150 us -> 147 us (0.980)
  waiting for transfers between devices: 18.8 us -> 17.1 us
  Pallas kernels: 62 us -> 60.5 us
where the time goes in v1:
time: 147 us
  Pallas kernels  60.5 us (41%)
  blocking collectives  33.3 us (23%)
  starting transfers between devices  32.1 us (22%)
  waiting for transfers between devices  17.1 us (12%)
  local copies, waits for them, and re-layouts  3.13 us (2%)
    pallas_call x6, Pallas kernels, attend(): pl.pallas_call(functools.partial(attention_kernel, pieces=len(kvs), first...  49.5 us
    all_to_all x1, blocking collectives, per_device(): lax.all_to_all(outgoing, PLANE, 0, 0, tiled=True)  33.3 us
    ppermute x8, starting transfers between devices, ring(): return lax.ppermute(x, axis, [(i, (i + by) % count) for i in range(count)])  19.6 us
    all_to_all x1, waiting for transfers between devices, per_device(): gathered = lax.all_to_all(banded, ('zl', 'x', 'zh', 'c'), 0, 0, tiled=True)  14.4 us
    pallas_call x1, Pallas kernels, project(): pl.pallas_call(project_kernel, in_specs=[pl.BlockSpec(memory_space=pltpu....  7.5 us
    ppermute x2, starting transfers between devices, later(): lax.ppermute(x, ('y', 'zl'), [(i, i + by) for i in range(count - by)])  7.17 us
    all_to_all x1, starting transfers between devices, per_device(): gathered = lax.all_to_all(banded, ('zl', 'x', 'zh', 'c'), 0, 0, tiled=True)  5.28 us
  transfers between devices with their start and end apart: 11, of which 2 were waited for; matrix products, arithmetic and copies ran while one was open for 0% of the time, Pallas kernels for 29%

profile of v1, /device:TPU:40, one launch (start us, length us, event | category | flops | bytes accessed | tf_op | source)
XLA Modules:
  0.0 146.7 jit_solution(14203458878944200976)
XLA Ops:
  0.0 0.0 copy-start
  0.0 1.3 bitcast_bitcast_fusion.2
  1.3 0.0 copy-done
  1.3 1.3 bitcast_bitcast_fusion
  2.6 0.3 pad_maximum_fusion
  2.9 33.3 %all_to_all.10 = bf16[16,160,384]{2,1,0:T(8,128)(2,1)S(1)} all-to-all(bf16[16,160,384]{2,1,0:T(8,128)(2,1)S(1)} %pad_maximum_fusion), channel_id=1, replica_groups=mesh['y'=4,'zl'=2,'x'=4,'zh'=2,'c'=2] {'zl','x','zh'}, dimensions={0} | all-to-all | bytes 3932160 | tf_op jit(solution)/shard_map/all_to_all | solution.py:351
  36.2 0.1 collective-permute-start.2
  36.3 0.1 fusion
  36.4 1.6 %collective-permute-start = (bf16[1280,256]{1,0:T(8,128)(2,1)S(1)}, bf16[1280,256]{1,0:T(8,128)(2,1)S(1)}, u32[]{:S(2)}, u32[]{:S(2)}) collective-permute-start(bf16[1280,256]{1,0:T(8,128)(2,1)S(1)} %get-tuple-element.19.refs_1_), channel_id=1, source_target_pairs={{0,32},{32,64},{64,96},{96,0},{1,33},{33,65},{65,97},{97,1},{2,34}... | collective-permute-start | bytes 1966088 | tf_op jit(solution)/shard_map/ppermute | solution.py:336
  38.0 0.5 collective-permute-start.1
  38.5 6.3 %shard_map.109.refs_3_ = f32[144,5120]{1,0:T(8,128)S(1)} custom-call(bf16[2560,128]{1,0:T(8,128)(2,1)S(1)} %slice.15.refs_0_, bf16[1280,256]{1,0:T(8,128)(2,1)S(1)} %get-tuple-element.19.refs_1_, bf16[1280,256]{1,0:T(8,128)(2,1)S(1)} %get-tuple-element.20.refs_2_), custom_call_target="tpu_custom_call" | custom-call | flops 5033164800 | bytes 4915200 | tf_op jit(solution)/shard_map/pallas_call | solution.py:133
  44.8 0.0 collective-permute-done.2.refs_0_
  44.8 14.3 %collective-permute-start.5 = (bf16[1280,256]{1,0:T(8,128)(2,1)S(1)}, bf16[1280,256]{1,0:T(8,128)(2,1)S(1)}, u32[]{:S(2)}, u32[]{:S(2)}) collective-permute-start(bf16[1280,256]{1,0:T(8,128)(2,1)S(1)} %get-tuple-element.20.refs_2_), channel_id=1, source_target_pairs={{0,32},{32,64},{64,96},{96,0},{1,33},{33,65},{65,97},{97,1},{2,34}... | collective-permute-start | bytes 1966088 | tf_op jit(solution)/shard_map/ppermute | solution.py:336
  59.1 0.0 collective-permute-start.6
  59.1 6.3 %shard_map.110.refs_3_ = f32[144,5120]{1,0:T(8,128)S(1)} custom-call(bf16[2560,128]{1,0:T(8,128)(2,1)S(1)} %collective-permute-done.2.refs_0_, bf16[1280,256]{1,0:T(8,128)(2,1)S(1)} %get-tuple-element.19.refs_1_, bf16[1280,256]{1,0:T(8,128)(2,1)S(1)} %get-tuple-element.20.refs_2_, f32[144,5120]{1,0:T(8,128)S(1)} %shard_map.109.refs_3_), custom_call_target="tpu_custom_call", output_to_operand_aliasing={{}: (3, {})} | custom-call | flops 5033164800 | bytes 4915200 | tf_op jit(solution)/shard_map/pallas_call | solution.py:133
  65.4 0.1 pad_maximum_fusion.1.refs_0_
  65.5 0.0 collective-permute-done.refs_1_
  65.5 0.0 collective-permute-done.1.refs_2_
  65.5 2.1 %collective-permute-start.3 = (bf16[1280,256]{1,0:T(8,128)(2,1)S(1)}, bf16[1280,256]{1,0:T(8,128)(2,1)S(1)}, u32[]{:S(2)}, u32[]{:S(2)}) collective-permute-start(bf16[1280,256]{1,0:T(8,128)(2,1)S(1)} %collective-permute-done.refs_1_), channel_id=1, source_target_pairs={{0,32},{32,64},{64,96},{96,0},{1,33},{33,65},{65,97},{97,1},{2,34}... | collective-permute-start | bytes 1966088 | tf_op jit(solution)/shard_map/ppermute | solution.py:336
  67.6 0.2 collective-permute-start.4
  67.8 12.2 %shard_map.111.refs_3_ = f32[144,5120]{1,0:T(8,128)S(1)} custom-call(bf16[5120,128]{1,0:T(8,128)(2,1)S(1)} %pad_maximum_fusion.1.refs_0_, bf16[1280,256]{1,0:T(8,128)(2,1)S(1)} %collective-permute-done.refs_1_, bf16[1280,256]{1,0:T(8,128)(2,1)S(1)} %collective-permute-done.1.refs_2_, f32[144,5120]{1,0:T(8,128)S(1)} %shard_map.110.refs_3_), custom_call_target="tpu_custom_call" | custom-call | flops 10066329600 | bytes 8519680 | tf_op jit(solution)/shard_map/pallas_call | solution.py:133
  80.0 0.0 collective-permute-done.5.refs_1_
  80.0 0.0 collective-permute-done.6.refs_2_
  80.0 12.2 %shard_map.112.refs_3_ = f32[144,5120]{1,0:T(8,128)S(1)} custom-call(bf16[5120,128]{1,0:T(8,128)(2,1)S(1)} %pad_maximum_fusion.1.refs_0_, bf16[1280,256]{1,0:T(8,128)(2,1)S(1)} %collective-permute-done.5.refs_1_, bf16[1280,256]{1,0:T(8,128)(2,1)S(1)} %collective-permute-done.6.refs_2_, f32[144,5120]{1,0:T(8,128)S(1)} %shard_map.111.refs_3_), custom_call_target="tpu_custom_call" | custom-call | flops 10066329600 | bytes 8519680 | tf_op jit(solution)/shard_map/pallas_call | solution.py:133
  92.2 0.0 collective-permute-done.3.refs_1_
  92.2 0.0 collective-permute-done.4.refs_2_
  92.2 6.3 %shard_map.114 = f32[144,2560]{1,0:T(8,128)S(1)} custom-call(bf16[2560,128]{1,0:T(8,128)(2,1)S(1)} %collective-permute-done.2.refs_0_, bf16[1280,256]{1,0:T(8,128)(2,1)S(1)} %collective-permute-done.3.refs_1_, bf16[1280,256]{1,0:T(8,128)(2,1)S(1)} %collective-permute-done.4.refs_2_, f32[144,5120]{1,0:T(8,128)S(1)} %shard_map.112.refs_3_), custom_call_target="tpu_custom_call" | custom-call | flops 5033164800 | bytes 4915200 | tf_op jit(solution)/shard_map/pallas_call | solution.py:133
  98.5 0.0 copy-start.1
  98.5 0.9 collective-permute-start.7
  99.4 6.2 %shard_map.113.mine_ref = f32[144,2560]{1,0:T(8,128)S(1)} custom-call(bf16[2560,128]{1,0:T(8,128)(2,1)S(1)} %slice.15.refs_0_, bf16[1280,256]{1,0:T(8,128)(2,1)S(1)} %collective-permute-done.3.refs_1_, bf16[1280,256]{1,0:T(8,128)(2,1)S(1)} %collective-permute-done.4.refs_2_, f32[144,5120]{1,0:T(8,128)S(1)} %shard_map.112.refs_3_), custom_call_target="tpu_custom_call" | custom-call | flops 5033164800 | bytes 4915200 | tf_op jit(solution)/shard_map/pallas_call | solution.py:133
  105.6 0.0 collective-permute-done.7.other_ref
  105.6 0.0 copy-done.1
  105.6 1.9 %shard_map.115 = bf16[32,112,128]{2,1,0:T(8,128)(2,1)} custom-call(f32[144,2560]{1,0:T(8,128)S(1)} %shard_map.113.mine_ref, f32[144,2560]{1,0:T(8,128)S(1)} %collective-permute-done.7.other_ref, bf16[896,640]{1,0:T(8,128)(2,1)S(1)} %copy-done.1), custom_call_target="tpu_custom_call" | custom-call | tf_op jit(solution)/shard_map/pallas_call | solution.py:184
  107.5 0.0 copy-start.6
  107.6 5.3 %all-to-all-start.1 = ((bf16[32,112,128]{2,1,0:T(8,128)(2,1)}), bf16[32,112,128]{2,1,0:T(8,128)(2,1)S(1)}, u32[]{:S(2)}, u32[]{:S(2)}) async-start(bf16[32,112,128]{2,1,0:T(8,128)(2,1)} %shard_map.115), calls=%async_computation.1 | async-start | bytes 1835008 | tf_op jit(solution)/shard_map/all_to_all | solution.py:374
  112.9 0.0 copy-done.7
  112.9 0.4 copy.16.final_ref
  113.3 14.4 %all-to-all-done.1 = bf16[32,112,128]{2,1,0:T(8,128)(2,1)S(1)} async-done(((bf16[32,112,128]{2,1,0:T(8,128)(2,1)}), bf16[32,112,128]{2,1,0:T(8,128)(2,1)S(1)}, u32[]{:S(2)}, u32[]{:S(2)}) %all-to-all-start.1) | async-done | bytes 917536 | tf_op jit(solution)/shard_map/all_to_all | solution.py:374
  127.7 0.0 copy-done.3
  127.7 0.0 copy-done.4
  127.7 0.0 copy-done.5
  127.7 0.0 copy-start.2
  127.7 7.5 %shard_map.116.now_ref = bf16[160,128]{1,0:T(8,128)(2,1)S(1)} custom-call(s32[1]{0:T(128)} %bitcast.1.band_ref, bf16[16,2,112,128]{3,2,1,0:T(8,128)(2,1)S(1)} %bitcast.31, bf16[2048,3072]{1,0:T(8,128)(2,1)} %w_ref.1, f32[1,3072]{1,0:T(1,128)S(1)} %bitcast.33, f32[1,3072]{1,0:T(1,128)S(1)} %bitcast.34, bf16[3072,64]{1,0:T(8,128)(2,1)S(1)} %copy.16.final_ref, ...), custom_call_target="tpu_custom_call" | custom-call | tf_op jit(solution)/shard_map/pallas_call | solution.py:263
  135.2 4.0 %collective-permute-start.8 = (bf16[160,128]{1,0:T(8,128)(2,1)S(1)}, bf16[160,128]{1,0:T(8,128)(2,1)S(1)}, u32[]{:S(2)}, u32[]{:S(2)}) collective-permute-start(bf16[160,128]{1,0:T(8,128)(2,1)S(1)} %shard_map.116.now_ref), channel_id=1, source_target_pairs={{0,16},{16,32},{32,48},{48,64},{64,80},{80,96},{96,112},{1,17},{17... | collective-permute-start | bytes 122888 | tf_op jit(solution)/shard_map/ppermute | solution.py:341
  139.2 3.2 %collective-permute-start.9 = (bf16[160,128]{1,0:T(8,128)(2,1)S(1)}, bf16[160,128]{1,0:T(8,128)(2,1)S(1)}, u32[]{:S(2)}, u32[]{:S(2)}) collective-permute-start(bf16[160,128]{1,0:T(8,128)(2,1)S(1)} %shard_map.116.now_ref), channel_id=1, source_target_pairs={{0,32},{16,48},{32,64},{48,80},{64,96},{80,112},{1,33},{17,49},{33... | collective-permute-start | bytes 122888 | tf_op jit(solution)/shard_map/ppermute | solution.py:341
  142.4 0.0 collective-permute-done.8.one_ref
  142.4 2.7 %collective-permute-done.9.two_ref = bf16[160,128]{1,0:T(8,128)(2,1)S(1)} collective-permute-done((bf16[160,128]{1,0:T(8,128)(2,1)S(1)}, bf16[160,128]{1,0:T(8,128)(2,1)S(1)}, u32[]{:S(2)}, u32[]{:S(2)}) %collective-permute-start.9) | collective-permute-done | bytes 40992 | tf_op jit(solution)/shard_map/ppermute | solution.py:341
  145.1 1.6 %shard_map.117 = bf16[10,64,512]{2,1,0:T(8,128)(2,1)} custom-call(s32[1]{0:T(128)} %bitcast.frame_ref, bf16[160,128]{1,0:T(8,128)(2,1)S(1)} %shard_map.116.now_ref, bf16[160,128]{1,0:T(8,128)(2,1)S(1)} %collective-permute-done.8.one_ref, bf16[160,128]{1,0:T(8,128)(2,1)S(1)} %collective-permute-done.9.two_ref, bf16[432,512]{1,0:T(8,128)(2,1)S(1)} %bitcast.32), custom_call_target="tpu_custom_call" | custom-call | tf_op jit(solution)/shard_map/pallas_call | solution.py:318
  (7 shorter events, 0.1 us)
Async XLA Ops:
  0.0 1.3 copy-start
  36.2 8.6 %collective-permute-start.2 = (bf16[2560,128]{1,0:T(8,128)(2,1)S(1)}, bf16[2560,128]{1,0:T(8,128)(2,1)S(1)}, u32[]{:S(2)}, u32[]{:S(2)}) collective-permute-start(bf16[2560,128]{1,0:T(8,128)(2,1)S(1)} %slice.15.refs_0_), channel_id=1, source_target_pairs={{0,1},{1,0},{2,3},{3,2},{4,5},{5,4},{6,7},{7,6},{8,9},{9,8},{10,11... | collective-permute-start | bytes 1966088 | tf_op jit(solution)/shard_map/ppermute | solution.py:336
  36.4 29.1 %collective-permute-start = (bf16[1280,256]{1,0:T(8,128)(2,1)S(1)}, bf16[1280,256]{1,0:T(8,128)(2,1)S(1)}, u32[]{:S(2)}, u32[]{:S(2)}) collective-permute-start(bf16[1280,256]{1,0:T(8,128)(2,1)S(1)} %get-tuple-element.19.refs_1_), channel_id=1, source_target_pairs={{0,32},{32,64},{64,96},{96,0},{1,33},{33,65},{65,97},{97,1},{2,34}... | collective-permute-start | bytes 1966088 | tf_op jit(solution)/shard_map/ppermute | solution.py:336
  38.0 27.4 %collective-permute-start.1 = (bf16[1280,256]{1,0:T(8,128)(2,1)S(1)}, bf16[1280,256]{1,0:T(8,128)(2,1)S(1)}, u32[]{:S(2)}, u32[]{:S(2)}) collective-permute-start(bf16[1280,256]{1,0:T(8,128)(2,1)S(1)} %get-tuple-element.20.refs_2_), channel_id=1, source_target_pairs={{0,96},{32,0},{64,32},{96,64},{1,97},{33,1},{65,33},{97,65},{2,98}... | collective-permute-start | bytes 1966088 | tf_op jit(solution)/shard_map/ppermute | solution.py:336
  44.8 35.2 %collective-permute-start.5 = (bf16[1280,256]{1,0:T(8,128)(2,1)S(1)}, bf16[1280,256]{1,0:T(8,128)(2,1)S(1)}, u32[]{:S(2)}, u32[]{:S(2)}) collective-permute-start(bf16[1280,256]{1,0:T(8,128)(2,1)S(1)} %get-tuple-element.20.refs_2_), channel_id=1, source_target_pairs={{0,32},{32,64},{64,96},{96,0},{1,33},{33,65},{65,97},{97,1},{2,34}... | collective-permute-start | bytes 1966088 | tf_op jit(solution)/shard_map/ppermute | solution.py:336
  59.1 20.9 %collective-permute-start.6 = (bf16[1280,256]{1,0:T(8,128)(2,1)S(1)}, bf16[1280,256]{1,0:T(8,128)(2,1)S(1)}, u32[]{:S(2)}, u32[]{:S(2)}) collective-permute-start(bf16[1280,256]{1,0:T(8,128)(2,1)S(1)} %get-tuple-element.19.refs_1_), channel_id=1, source_target_pairs={{0,96},{32,0},{64,32},{96,64},{1,97},{33,1},{65,33},{97,65},{2,98}... | collective-permute-start | bytes 1966088 | tf_op jit(solution)/shard_map/ppermute | solution.py:336
  65.5 26.7 %collective-permute-start.3 = (bf16[1280,256]{1,0:T(8,128)(2,1)S(1)}, bf16[1280,256]{1,0:T(8,128)(2,1)S(1)}, u32[]{:S(2)}, u32[]{:S(2)}) collective-permute-start(bf16[1280,256]{1,0:T(8,128)(2,1)S(1)} %collective-permute-done.refs_1_), channel_id=1, source_target_pairs={{0,32},{32,64},{64,96},{96,0},{1,33},{33,65},{65,97},{97,1},{2,34}... | collective-permute-start | bytes 1966088 | tf_op jit(solution)/shard_map/ppermute | solution.py:336
  67.6 24.6 %collective-permute-start.4 = (bf16[1280,256]{1,0:T(8,128)(2,1)S(1)}, bf16[1280,256]{1,0:T(8,128)(2,1)S(1)}, u32[]{:S(2)}, u32[]{:S(2)}) collective-permute-start(bf16[1280,256]{1,0:T(8,128)(2,1)S(1)} %collective-permute-done.1.refs_2_), channel_id=1, source_target_pairs={{0,96},{32,0},{64,32},{96,64},{1,97},{33,1},{65,33},{97,65},{2,98}... | collective-permute-start | bytes 1966088 | tf_op jit(solution)/shard_map/ppermute | solution.py:336
  98.5 7.1 %copy-start.1 = (bf16[896,640]{1,0:T(8,128)(2,1)S(1)}, bf16[896,640]{1,0:T(8,128)(2,1)}, u32[]{:S(2)}) copy-start(bf16[896,640]{1,0:T(8,128)(2,1)} %constant.29.clone.choose_ref) | copy-start | bytes 3440644
  98.5 7.1 %collective-permute-start.7 = (f32[144,2560]{1,0:T(8,128)S(1)}, f32[144,2560]{1,0:T(8,128)S(1)}, u32[]{:S(2)}, u32[]{:S(2)}) collective-permute-start(f32[144,2560]{1,0:T(8,128)S(1)} %shard_map.114), channel_id=1, source_target_pairs={{0,1},{1,0},{2,3},{3,2},{4,5},{5,4},{6,7},{7,6},{8,9},{9,8},{10,11... | collective-permute-start | bytes 4423688 | tf_op jit(solution)/shard_map/ppermute | solution.py:336
  107.5 5.3 %copy-start.7 = (bf16[3072,64]{0,1:T(8,128)(2,1)S(1)}, bf16[3072,64]{0,1:T(8,128)(2,1)}, u32[]{:S(2)}) copy-start(bf16[3072,64]{0,1:T(8,128)(2,1)} %param.17) | copy-start | bytes 1179652
  107.5 20.1 %copy-start.3 = (bf16[160,160]{1,0:T(8,128)(2,1)S(1)}, bf16[160,160]{1,0:T(8,128)(2,1)}, u32[]{:S(2)}) copy-start(bf16[160,160]{1,0:T(8,128)(2,1)} %constant.31.clone.order_ref) | copy-start | bytes 153604
  107.5 20.1 %copy-start.4 = (bf16[3,64,128]{2,1,0:T(8,128)(2,1)S(1)}, bf16[3,64,128]{2,1,0:T(8,128)(2,1)}, u32[]{:S(2)}) copy-start(bf16[3,64,128]{2,1,0:T(8,128)(2,1)} %constant.30.clone.choose_ref) | copy-start | bytes 147460
  107.5 20.1 %copy-start.5 = (f32[3072]{0:T(1024)S(1)}, f32[3072]{0:T(1024)}, u32[]{:S(2)}) copy-start(f32[3072]{0:T(1024)} %param.15) | copy-start | bytes 36868
  107.5 20.1 %copy-start.6 = (f32[3072]{0:T(1024)S(1)}, f32[3072]{0:T(1024)}, u32[]{:S(2)}) copy-start(f32[3072]{0:T(1024)} %param.16) | copy-start | bytes 36868
  107.6 20.1 %all-to-all-start.1 = ((bf16[32,112,128]{2,1,0:T(8,128)(2,1)}), bf16[32,112,128]{2,1,0:T(8,128)(2,1)S(1)}, u32[]{:S(2)}, u32[]{:S(2)}) async-start(bf16[32,112,128]{2,1,0:T(8,128)(2,1)} %shard_map.115), calls=%async_computation.1 | async-start | bytes 1835008 | tf_op jit(solution)/shard_map/all_to_all | solution.py:374
  127.7 17.4 %copy-start.2 = (bf16[3,3,3,16,512]{4,3,2,1,0:T(8,128)(2,1)S(1)}, bf16[3,3,3,16,512]{4,3,2,1,0:T(8,128)(2,1)}, u32[]{:S(2)}) copy-start(bf16[3,3,3,16,512]{4,3,2,1,0:T(8,128)(2,1)} %param.18) | copy-start | bytes 1327108
  135.2 7.2 %collective-permute-start.8 = (bf16[160,128]{1,0:T(8,128)(2,1)S(1)}, bf16[160,128]{1,0:T(8,128)(2,1)S(1)}, u32[]{:S(2)}, u32[]{:S(2)}) collective-permute-start(bf16[160,128]{1,0:T(8,128)(2,1)S(1)} %shard_map.116.now_ref), channel_id=1, source_target_pairs={{0,16},{16,32},{32,48},{48,64},{64,80},{80,96},{96,112},{1,17},{17... | collective-permute-start | bytes 122888 | tf_op jit(solution)/shard_map/ppermute | solution.py:341
  139.2 5.9 %collective-permute-start.9 = (bf16[160,128]{1,0:T(8,128)(2,1)S(1)}, bf16[160,128]{1,0:T(8,128)(2,1)S(1)}, u32[]{:S(2)}, u32[]{:S(2)}) collective-permute-start(bf16[160,128]{1,0:T(8,128)(2,1)S(1)} %shard_map.116.now_ref), channel_id=1, source_target_pairs={{0,32},{16,48},{32,64},{48,80},{64,96},{80,112},{1,33},{17,49},{33... | collective-permute-start | bytes 122888 | tf_op jit(solution)/shard_map/ppermute | solution.py:341

commit v2 on v1

--- a/solution.py
+++ b/solution.py
@@ -34,8 +34,9 @@
     return lax.dot_general(a, b, NT, preferred_element_type=jnp.float32)
 
 
-def attention_kernel(*refs, pieces, first, filled):
-    q_ref = refs[0]
+def attention_kernel(*refs, pieces, first, filled, block, read, write):
+    here = pl.multiple_of(pl.program_id(0) * block, block)
+    q_ref = refs[0].at[pl.ds(here, block)]
     kv_refs = refs[1 : 1 + pieces]
     rest = refs[1 + pieces :]
     if filled:
@@ -44,15 +45,11 @@
         out_ref, keys_ref, vt_ref = rest
     else:
         in_ref, out_ref, keys_ref, vt_ref = rest
+        in_ref = in_ref.at[:, pl.ds(pl.multiple_of(read + here, block), block)]
+    out_ref = out_ref.at[:, pl.ds(pl.multiple_of(write + here, block), block)]
     starts = [0]
     for kv in kv_refs:
         starts.append(starts[-1] + kv.shape[0])
-
-    @pl.when(pl.program_id(0) == 0)
-    def _():
-        for n, kv in enumerate(kv_refs):
-            keys_ref[starts[n] : starts[n + 1], :] = kv[:, :HD]
-            vt_ref[:, starts[n] : starts[n + 1]] = kv[:, HD:].T
 
     q_scaled = q_ref[...].astype(jnp.float32) * SCALE_LOG2
     q_hi = q_scaled.astype(jnp.bfloat16)
@@ -78,7 +75,7 @@
             weights = jnp.exp2(scores_of(kv[at : at + step, :HD]) - reference)
             total = total + jnp.sum(weights.reshape(step // 8, 8, cols), axis=0)
             acc = acc + jnp.dot(
-                vt_ref[:, starts[n] + at : starts[n] + at + step],
+                kv[at : at + step, HD:].T,
                 weights.astype(jnp.bfloat16),
                 preferred_element_type=jnp.float32,
             )
@@ -93,6 +90,9 @@
             out_ref[0 : HD + 8, :] = jnp.zeros((HD + 8, cols), jnp.float32)
         else:
             out_ref[...] = in_ref[...]
+        for n, kv in enumerate(kv_refs):
+            keys_ref[starts[n] : starts[n + 1], :] = kv[:, :HD]
+            vt_ref[:, starts[n] : starts[n + 1]] = kv[:, HD:].T
 
         def absorb(i, carry):
             at = pl.multiple_of(i * 128, 128)
@@ -119,22 +119,27 @@
     keys = sum(kv.shape[0] for kv in kvs)
     shift = offset // block
     write = shift if columns else 0
-    in_specs = [pl.BlockSpec((block, HD), lambda i: (i, 0))]
-    in_specs += [pl.BlockSpec(kv.shape, lambda i: (0, 0)) for kv in kvs]
+    vmem = pl.BlockSpec(memory_space=pltpu.VMEM)
     args = [q] + list(kvs)
     aliases = {}
     if not first:
-        in_specs.append(pl.BlockSpec((STATE, block), lambda i: (0, i + shift)))
         args.append(state)
     if fill is not None:
         aliases = {len(args): 0}
-        in_specs.append(pl.BlockSpec(memory_space=pl.ANY))
         args.append(fill)
     return pl.pallas_call(
-        functools.partial(attention_kernel, pieces=len(kvs), first=first, filled=fill is not None),
+        functools.partial(
+            attention_kernel,
+            pieces=len(kvs),
+            first=first,
+            filled=fill is not None,
+            block=block,
+            read=shift * block,
+            write=write * block,
+        ),
         grid=(rows // block,),
-        in_specs=in_specs,
-        out_specs=pl.BlockSpec((STATE, block), lambda i: (0, i + write)),
+        in_specs=[vmem] * len(args),
+        out_specs=vmem,
         out_shape=jax.ShapeDtypeStruct((STATE, columns or rows), jnp.float32),
         scratch_shapes=[pltpu.VMEM((keys, HD), jnp.bfloat16), pltpu.VMEM((HD, keys), jnp.bfloat16)],
         input_output_aliases=aliases,

time: 147 us -> 145 us (0.986)
  Pallas kernels: 60.5 us -> 57.7 us
    pallas_call x6, Pallas kernels: 49.5 us -> 46.7 us  [attend(): pl.pallas_call(functools.partial(attention_kernel, pieces=len(kvs), first...]
  transfers between devices with their start and end apart: 11 -> 11, of which waited for: 2 -> 2; matrix products, arithmetic and copies ran while one was open for 0% -> 0% of each run, Pallas kernels for 29% -> 28%
where the time goes in v2:
time: 145 us; the launch traced here: 144 us
  Pallas kernels  57.7 us (40%)
  blocking collectives  33.3 us (23%)
  starting transfers between devices  32.2 us (22%)
  waiting for transfers between devices  17.1 us (12%)
  local copies, waits for them, and re-layouts  3.13 us (2%)
    pallas_call x6, Pallas kernels, attend(): pl.pallas_call(functools.partial(attention_kernel, pieces=len(kvs), first...  46.7 us
    all_to_all x1, blocking collectives, per_device(): lax.all_to_all(outgoing, PLANE, 0, 0, tiled=True)  33.3 us
    ppermute x8, starting transfers between devices, ring(): return lax.ppermute(x, axis, [(i, (i + by) % count) for i in range(count)])  19.9 us
    all_to_all x1, waiting for transfers between devices, per_device(): gathered = lax.all_to_all(banded, ('zl', 'x', 'zh', 'c'), 0, 0, tiled=True)  14.4 us
    pallas_call x1, Pallas kernels, project(): pl.pallas_call(project_kernel, in_specs=[pl.BlockSpec(memory_space=pltpu....  7.5 us
    ppermute x2, starting transfers between devices, later(): lax.ppermute(x, ('y', 'zl'), [(i, i + by) for i in range(count - by)])  7.09 us
    all_to_all x1, starting transfers between devices, per_device(): gathered = lax.all_to_all(banded, ('zl', 'x', 'zh', 'c'), 0, 0, tiled=True)  5.28 us
  transfers between devices with their start and end apart: 11, of which 2 were waited for; matrix products, arithmetic and copies ran while one was open for 0% of the time, Pallas kernels for 28%

profile of v2, /device:TPU:40, one launch (start us, length us, event | category | flops | bytes accessed | tf_op | source)
XLA Modules:
  0.0 144.2 jit_solution(8465181192180096092)
XLA Ops:
  0.0 0.0 copy-start
  0.0 1.3 bitcast_bitcast_fusion.2
  1.3 0.0 copy-done
  1.3 1.3 bitcast_bitcast_fusion
  2.6 0.3 pad_maximum_fusion
  2.9 33.3 %all_to_all.10 = bf16[16,160,384]{2,1,0:T(8,128)(2,1)S(1)} all-to-all(bf16[16,160,384]{2,1,0:T(8,128)(2,1)S(1)} %pad_maximum_fusion), channel_id=1, replica_groups=mesh['y'=4,'zl'=2,'x'=4,'zh'=2,'c'=2] {'zl','x','zh'}, dimensions={0} | all-to-all | bytes 3932160 | tf_op jit(solution)/shard_map/all_to_all | solution.py:356
  36.2 0.1 collective-permute-start.2
  36.3 0.1 fusion
  36.4 1.6 %collective-permute-start = (bf16[1280,256]{1,0:T(8,128)(2,1)S(1)}, bf16[1280,256]{1,0:T(8,128)(2,1)S(1)}, u32[]{:S(2)}, u32[]{:S(2)}) collective-permute-start(bf16[1280,256]{1,0:T(8,128)(2,1)S(1)} %get-tuple-element.19.refs_1_), channel_id=1, source_target_pairs={{0,32},{32,64},{64,96},{96,0},{1,33},{33,65},{65,97},{97,1},{2,34}... | collective-permute-start | bytes 1966088 | tf_op jit(solution)/shard_map/ppermute | solution.py:341
  38.0 0.5 collective-permute-start.1
  38.5 5.9 %shard_map.109.refs_3_ = f32[144,5120]{1,0:T(8,128)S(1)} custom-call(bf16[2560,128]{1,0:T(8,128)(2,1)S(1)} %slice.15.refs_0_, bf16[1280,256]{1,0:T(8,128)(2,1)S(1)} %get-tuple-element.19.refs_1_, bf16[1280,256]{1,0:T(8,128)(2,1)S(1)} %get-tuple-element.20.refs_2_), custom_call_target="tpu_custom_call" | custom-call | flops 5033164800 | bytes 4915200 | tf_op jit(solution)/shard_map/pallas_call | solution.py:130
  44.4 0.0 collective-permute-done.2.refs_0_
  44.5 14.4 %collective-permute-start.5 = (bf16[1280,256]{1,0:T(8,128)(2,1)S(1)}, bf16[1280,256]{1,0:T(8,128)(2,1)S(1)}, u32[]{:S(2)}, u32[]{:S(2)}) collective-permute-start(bf16[1280,256]{1,0:T(8,128)(2,1)S(1)} %get-tuple-element.20.refs_2_), channel_id=1, source_target_pairs={{0,32},{32,64},{64,96},{96,0},{1,33},{33,65},{65,97},{97,1},{2,34}... | collective-permute-start | bytes 1966088 | tf_op jit(solution)/shard_map/ppermute | solution.py:341
  58.9 0.0 collective-permute-start.6
  58.9 5.9 %shard_map.110.refs_3_ = f32[144,5120]{1,0:T(8,128)S(1)} custom-call(bf16[2560,128]{1,0:T(8,128)(2,1)S(1)} %collective-permute-done.2.refs_0_, bf16[1280,256]{1,0:T(8,128)(2,1)S(1)} %get-tuple-element.19.refs_1_, bf16[1280,256]{1,0:T(8,128)(2,1)S(1)} %get-tuple-element.20.refs_2_, f32[144,5120]{1,0:T(8,128)S(1)} %shard_map.109.refs_3_), custom_call_target="tpu_custom_call", output_to_operand_aliasing={{}: (3, {})} | custom-call | flops 5033164800 | bytes 4915200 | tf_op jit(solution)/shard_map/pallas_call | solution.py:130
  64.8 0.1 pad_maximum_fusion.1.refs_0_
  64.9 0.0 collective-permute-done.refs_1_
  64.9 0.0 collective-permute-done.1.refs_2_
  64.9 2.1 %collective-permute-start.3 = (bf16[1280,256]{1,0:T(8,128)(2,1)S(1)}, bf16[1280,256]{1,0:T(8,128)(2,1)S(1)}, u32[]{:S(2)}, u32[]{:S(2)}) collective-permute-start(bf16[1280,256]{1,0:T(8,128)(2,1)S(1)} %collective-permute-done.refs_1_), channel_id=1, source_target_pairs={{0,32},{32,64},{64,96},{96,0},{1,33},{33,65},{65,97},{97,1},{2,34}... | collective-permute-start | bytes 1966088 | tf_op jit(solution)/shard_map/ppermute | solution.py:341
  67.0 0.2 collective-permute-start.4
  67.2 11.6 %shard_map.111.refs_3_ = f32[144,5120]{1,0:T(8,128)S(1)} custom-call(bf16[5120,128]{1,0:T(8,128)(2,1)S(1)} %pad_maximum_fusion.1.refs_0_, bf16[1280,256]{1,0:T(8,128)(2,1)S(1)} %collective-permute-done.refs_1_, bf16[1280,256]{1,0:T(8,128)(2,1)S(1)} %collective-permute-done.1.refs_2_, f32[144,5120]{1,0:T(8,128)S(1)} %shard_map.110.refs_3_), custom_call_target="tpu_custom_call" | custom-call | flops 10066329600 | bytes 8519680 | tf_op jit(solution)/shard_map/pallas_call | solution.py:130
  78.8 0.0 collective-permute-done.5.refs_1_
  78.9 0.0 collective-permute-done.6.refs_2_
  78.9 11.6 %shard_map.112.refs_3_ = f32[144,5120]{1,0:T(8,128)S(1)} custom-call(bf16[5120,128]{1,0:T(8,128)(2,1)S(1)} %pad_maximum_fusion.1.refs_0_, bf16[1280,256]{1,0:T(8,128)(2,1)S(1)} %collective-permute-done.5.refs_1_, bf16[1280,256]{1,0:T(8,128)(2,1)S(1)} %collective-permute-done.6.refs_2_, f32[144,5120]{1,0:T(8,128)S(1)} %shard_map.111.refs_3_), custom_call_target="tpu_custom_call" | custom-call | flops 10066329600 | bytes 8519680 | tf_op jit(solution)/shard_map/pallas_call | solution.py:130
  90.5 0.0 collective-permute-done.3.refs_1_
  90.5 0.0 collective-permute-done.4.refs_2_
  90.5 5.8 %shard_map.114 = f32[144,2560]{1,0:T(8,128)S(1)} custom-call(bf16[2560,128]{1,0:T(8,128)(2,1)S(1)} %collective-permute-done.2.refs_0_, bf16[1280,256]{1,0:T(8,128)(2,1)S(1)} %collective-permute-done.3.refs_1_, bf16[1280,256]{1,0:T(8,128)(2,1)S(1)} %collective-permute-done.4.refs_2_, f32[144,5120]{1,0:T(8,128)S(1)} %shard_map.112.refs_3_), custom_call_target="tpu_custom_call" | custom-call | flops 5033164800 | bytes 4915200 | tf_op jit(solution)/shard_map/pallas_call | solution.py:130
  96.3 0.0 copy-start.1
  96.4 1.0 collective-permute-start.7
  97.3 5.8 %shard_map.113.mine_ref = f32[144,2560]{1,0:T(8,128)S(1)} custom-call(bf16[2560,128]{1,0:T(8,128)(2,1)S(1)} %slice.15.refs_0_, bf16[1280,256]{1,0:T(8,128)(2,1)S(1)} %collective-permute-done.3.refs_1_, bf16[1280,256]{1,0:T(8,128)(2,1)S(1)} %collective-permute-done.4.refs_2_, f32[144,5120]{1,0:T(8,128)S(1)} %shard_map.112.refs_3_), custom_call_target="tpu_custom_call" | custom-call | flops 5033164800 | bytes 4915200 | tf_op jit(solution)/shard_map/pallas_call | solution.py:130
  103.1 0.0 collective-permute-done.7.other_ref
  103.1 0.0 copy-done.1
  103.1 1.9 %shard_map.115 = bf16[32,112,128]{2,1,0:T(8,128)(2,1)} custom-call(f32[144,2560]{1,0:T(8,128)S(1)} %shard_map.113.mine_ref, f32[144,2560]{1,0:T(8,128)S(1)} %collective-permute-done.7.other_ref, bf16[896,640]{1,0:T(8,128)(2,1)S(1)} %copy-done.1), custom_call_target="tpu_custom_call" | custom-call | tf_op jit(solution)/shard_map/pallas_call | solution.py:189
  105.0 0.0 copy-start.6
  105.1 5.3 %all-to-all-start.1 = ((bf16[32,112,128]{2,1,0:T(8,128)(2,1)}), bf16[32,112,128]{2,1,0:T(8,128)(2,1)S(1)}, u32[]{:S(2)}, u32[]{:S(2)}) async-start(bf16[32,112,128]{2,1,0:T(8,128)(2,1)} %shard_map.115), calls=%async_computation.1 | async-start | bytes 1835008 | tf_op jit(solution)/shard_map/all_to_all | solution.py:379
  110.4 0.0 copy-done.7
  110.4 0.4 copy.16.final_ref
  110.8 14.4 %all-to-all-done.1 = bf16[32,112,128]{2,1,0:T(8,128)(2,1)S(1)} async-done(((bf16[32,112,128]{2,1,0:T(8,128)(2,1)}), bf16[32,112,128]{2,1,0:T(8,128)(2,1)S(1)}, u32[]{:S(2)}, u32[]{:S(2)}) %all-to-all-start.1) | async-done | bytes 917536 | tf_op jit(solution)/shard_map/all_to_all | solution.py:379
  125.2 0.0 copy-done.3
  125.2 0.0 copy-done.4
  125.2 0.0 copy-done.5
  125.2 0.0 copy-start.2
  125.2 7.5 %shard_map.116.now_ref = bf16[160,128]{1,0:T(8,128)(2,1)S(1)} custom-call(s32[1]{0:T(128)} %bitcast.1.band_ref, bf16[16,2,112,128]{3,2,1,0:T(8,128)(2,1)S(1)} %bitcast.31, bf16[2048,3072]{1,0:T(8,128)(2,1)} %w_ref.1, f32[1,3072]{1,0:T(1,128)S(1)} %bitcast.33, f32[1,3072]{1,0:T(1,128)S(1)} %bitcast.34, bf16[3072,64]{1,0:T(8,128)(2,1)S(1)} %copy.16.final_ref, ...), custom_call_target="tpu_custom_call" | custom-call | tf_op jit(solution)/shard_map/pallas_call | solution.py:268
  132.7 3.9 %collective-permute-start.8 = (bf16[160,128]{1,0:T(8,128)(2,1)S(1)}, bf16[160,128]{1,0:T(8,128)(2,1)S(1)}, u32[]{:S(2)}, u32[]{:S(2)}) collective-permute-start(bf16[160,128]{1,0:T(8,128)(2,1)S(1)} %shard_map.116.now_ref), channel_id=1, source_target_pairs={{0,16},{16,32},{32,48},{48,64},{64,80},{80,96},{96,112},{1,17},{17... | collective-permute-start | bytes 122888 | tf_op jit(solution)/shard_map/ppermute | solution.py:346
  136.6 3.2 %collective-permute-start.9 = (bf16[160,128]{1,0:T(8,128)(2,1)S(1)}, bf16[160,128]{1,0:T(8,128)(2,1)S(1)}, u32[]{:S(2)}, u32[]{:S(2)}) collective-permute-start(bf16[160,128]{1,0:T(8,128)(2,1)S(1)} %shard_map.116.now_ref), channel_id=1, source_target_pairs={{0,32},{16,48},{32,64},{48,80},{64,96},{80,112},{1,33},{17,49},{33... | collective-permute-start | bytes 122888 | tf_op jit(solution)/shard_map/ppermute | solution.py:346
  139.8 0.0 collective-permute-done.8.one_ref
  139.8 2.7 %collective-permute-done.9.two_ref = bf16[160,128]{1,0:T(8,128)(2,1)S(1)} collective-permute-done((bf16[160,128]{1,0:T(8,128)(2,1)S(1)}, bf16[160,128]{1,0:T(8,128)(2,1)S(1)}, u32[]{:S(2)}, u32[]{:S(2)}) %collective-permute-start.9) | collective-permute-done | bytes 40992 | tf_op jit(solution)/shard_map/ppermute | solution.py:346
  142.5 1.6 %shard_map.117 = bf16[10,64,512]{2,1,0:T(8,128)(2,1)} custom-call(s32[1]{0:T(128)} %bitcast.frame_ref, bf16[160,128]{1,0:T(8,128)(2,1)S(1)} %shard_map.116.now_ref, bf16[160,128]{1,0:T(8,128)(2,1)S(1)} %collective-permute-done.8.one_ref, bf16[160,128]{1,0:T(8,128)(2,1)S(1)} %collective-permute-done.9.two_ref, bf16[432,512]{1,0:T(8,128)(2,1)S(1)} %bitcast.32), custom_call_target="tpu_custom_call" | custom-call | tf_op jit(solution)/shard_map/pallas_call | solution.py:323
  (7 shorter events, 0.1 us)
Async XLA Ops:
  0.0 1.3 copy-start
  36.2 8.2 %collective-permute-start.2 = (bf16[2560,128]{1,0:T(8,128)(2,1)S(1)}, bf16[2560,128]{1,0:T(8,128)(2,1)S(1)}, u32[]{:S(2)}, u32[]{:S(2)}) collective-permute-start(bf16[2560,128]{1,0:T(8,128)(2,1)S(1)} %slice.15.refs_0_), channel_id=1, source_target_pairs={{0,1},{1,0},{2,3},{3,2},{4,5},{5,4},{6,7},{7,6},{8,9},{9,8},{10,11... | collective-permute-start | bytes 1966088 | tf_op jit(solution)/shard_map/ppermute | solution.py:341
  36.4 28.5 %collective-permute-start = (bf16[1280,256]{1,0:T(8,128)(2,1)S(1)}, bf16[1280,256]{1,0:T(8,128)(2,1)S(1)}, u32[]{:S(2)}, u32[]{:S(2)}) collective-permute-start(bf16[1280,256]{1,0:T(8,128)(2,1)S(1)} %get-tuple-element.19.refs_1_), channel_id=1, source_target_pairs={{0,32},{32,64},{64,96},{96,0},{1,33},{33,65},{65,97},{97,1},{2,34}... | collective-permute-start | bytes 1966088 | tf_op jit(solution)/shard_map/ppermute | solution.py:341
  38.0 26.9 %collective-permute-start.1 = (bf16[1280,256]{1,0:T(8,128)(2,1)S(1)}, bf16[1280,256]{1,0:T(8,128)(2,1)S(1)}, u32[]{:S(2)}, u32[]{:S(2)}) collective-permute-start(bf16[1280,256]{1,0:T(8,128)(2,1)S(1)} %get-tuple-element.20.refs_2_), channel_id=1, source_target_pairs={{0,96},{32,0},{64,32},{96,64},{1,97},{33,1},{65,33},{97,65},{2,98}... | collective-permute-start | bytes 1966088 | tf_op jit(solution)/shard_map/ppermute | solution.py:341
  44.5 34.4 %collective-permute-start.5 = (bf16[1280,256]{1,0:T(8,128)(2,1)S(1)}, bf16[1280,256]{1,0:T(8,128)(2,1)S(1)}, u32[]{:S(2)}, u32[]{:S(2)}) collective-permute-start(bf16[1280,256]{1,0:T(8,128)(2,1)S(1)} %get-tuple-element.20.refs_2_), channel_id=1, source_target_pairs={{0,32},{32,64},{64,96},{96,0},{1,33},{33,65},{65,97},{97,1},{2,34}... | collective-permute-start | bytes 1966088 | tf_op jit(solution)/shard_map/ppermute | solution.py:341
  58.9 20.0 %collective-permute-start.6 = (bf16[1280,256]{1,0:T(8,128)(2,1)S(1)}, bf16[1280,256]{1,0:T(8,128)(2,1)S(1)}, u32[]{:S(2)}, u32[]{:S(2)}) collective-permute-start(bf16[1280,256]{1,0:T(8,128)(2,1)S(1)} %get-tuple-element.19.refs_1_), channel_id=1, source_target_pairs={{0,96},{32,0},{64,32},{96,64},{1,97},{33,1},{65,33},{97,65},{2,98}... | collective-permute-start | bytes 1966088 | tf_op jit(solution)/shard_map/ppermute | solution.py:341
  64.9 25.5 %collective-permute-start.3 = (bf16[1280,256]{1,0:T(8,128)(2,1)S(1)}, bf16[1280,256]{1,0:T(8,128)(2,1)S(1)}, u32[]{:S(2)}, u32[]{:S(2)}) collective-permute-start(bf16[1280,256]{1,0:T(8,128)(2,1)S(1)} %collective-permute-done.refs_1_), channel_id=1, source_target_pairs={{0,32},{32,64},{64,96},{96,0},{1,33},{33,65},{65,97},{97,1},{2,34}... | collective-permute-start | bytes 1966088 | tf_op jit(solution)/shard_map/ppermute | solution.py:341
  67.0 23.5 %collective-permute-start.4 = (bf16[1280,256]{1,0:T(8,128)(2,1)S(1)}, bf16[1280,256]{1,0:T(8,128)(2,1)S(1)}, u32[]{:S(2)}, u32[]{:S(2)}) collective-permute-start(bf16[1280,256]{1,0:T(8,128)(2,1)S(1)} %collective-permute-done.1.refs_2_), channel_id=1, source_target_pairs={{0,96},{32,0},{64,32},{96,64},{1,97},{33,1},{65,33},{97,65},{2,98}... | collective-permute-start | bytes 1966088 | tf_op jit(solution)/shard_map/ppermute | solution.py:341
  96.3 6.8 %copy-start.1 = (bf16[896,640]{1,0:T(8,128)(2,1)S(1)}, bf16[896,640]{1,0:T(8,128)(2,1)}, u32[]{:S(2)}) copy-start(bf16[896,640]{1,0:T(8,128)(2,1)} %constant.29.clone.choose_ref) | copy-start | bytes 3440644
  96.4 6.8 %collective-permute-start.7 = (f32[144,2560]{1,0:T(8,128)S(1)}, f32[144,2560]{1,0:T(8,128)S(1)}, u32[]{:S(2)}, u32[]{:S(2)}) collective-permute-start(f32[144,2560]{1,0:T(8,128)S(1)} %shard_map.114), channel_id=1, source_target_pairs={{0,1},{1,0},{2,3},{3,2},{4,5},{5,4},{6,7},{7,6},{8,9},{9,8},{10,11... | collective-permute-start | bytes 4423688 | tf_op jit(solution)/shard_map/ppermute | solution.py:341
  105.0 5.3 %copy-start.7 = (bf16[3072,64]{0,1:T(8,128)(2,1)S(1)}, bf16[3072,64]{0,1:T(8,128)(2,1)}, u32[]{:S(2)}) copy-start(bf16[3072,64]{0,1:T(8,128)(2,1)} %param.17) | copy-start | bytes 1179652
  105.0 20.1 %copy-start.3 = (bf16[160,160]{1,0:T(8,128)(2,1)S(1)}, bf16[160,160]{1,0:T(8,128)(2,1)}, u32[]{:S(2)}) copy-start(bf16[160,160]{1,0:T(8,128)(2,1)} %constant.31.clone.order_ref) | copy-start | bytes 153604
  105.0 20.1 %copy-start.4 = (bf16[3,64,128]{2,1,0:T(8,128)(2,1)S(1)}, bf16[3,64,128]{2,1,0:T(8,128)(2,1)}, u32[]{:S(2)}) copy-start(bf16[3,64,128]{2,1,0:T(8,128)(2,1)} %constant.30.clone.choose_ref) | copy-start | bytes 147460
  105.0 20.1 %copy-start.5 = (f32[3072]{0:T(1024)S(1)}, f32[3072]{0:T(1024)}, u32[]{:S(2)}) copy-start(f32[3072]{0:T(1024)} %param.15) | copy-start | bytes 36868
  105.0 20.1 %copy-start.6 = (f32[3072]{0:T(1024)S(1)}, f32[3072]{0:T(1024)}, u32[]{:S(2)}) copy-start(f32[3072]{0:T(1024)} %param.16) | copy-start | bytes 36868
  105.1 20.1 %all-to-all-start.1 = ((bf16[32,112,128]{2,1,0:T(8,128)(2,1)}), bf16[32,112,128]{2,1,0:T(8,128)(2,1)S(1)}, u32[]{:S(2)}, u32[]{:S(2)}) async-start(bf16[32,112,128]{2,1,0:T(8,128)(2,1)} %shard_map.115), calls=%async_computation.1 | async-start | bytes 1835008 | tf_op jit(solution)/shard_map/all_to_all | solution.py:379
  125.2 17.3 %copy-start.2 = (bf16[3,3,3,16,512]{4,3,2,1,0:T(8,128)(2,1)S(1)}, bf16[3,3,3,16,512]{4,3,2,1,0:T(8,128)(2,1)}, u32[]{:S(2)}) copy-start(bf16[3,3,3,16,512]{4,3,2,1,0:T(8,128)(2,1)} %param.18) | copy-start | bytes 1327108
  132.7 7.1 %collective-permute-start.8 = (bf16[160,128]{1,0:T(8,128)(2,1)S(1)}, bf16[160,128]{1,0:T(8,128)(2,1)S(1)}, u32[]{:S(2)}, u32[]{:S(2)}) collective-permute-start(bf16[160,128]{1,0:T(8,128)(2,1)S(1)} %shard_map.116.now_ref), channel_id=1, source_target_pairs={{0,16},{16,32},{32,48},{48,64},{64,80},{80,96},{96,112},{1,17},{17... | collective-permute-start | bytes 122888 | tf_op jit(solution)/shard_map/ppermute | solution.py:346
  136.6 5.9 %collective-permute-start.9 = (bf16[160,128]{1,0:T(8,128)(2,1)S(1)}, bf16[160,128]{1,0:T(8,128)(2,1)S(1)}, u32[]{:S(2)}, u32[]{:S(2)}) collective-permute-start(bf16[160,128]{1,0:T(8,128)(2,1)S(1)} %shard_map.116.now_ref), channel_id=1, source_target_pairs={{0,32},{16,48},{32,64},{48,80},{64,96},{80,112},{1,33},{17,49},{33... | collective-permute-start | bytes 122888 | tf_op jit(solution)/shard_map/ppermute | solution.py:346

commit v3 on v2

--- a/solution.py
+++ b/solution.py
@@ -213,6 +213,7 @@
 
 
 TILE_N = 512
+AHEAD = 4
 
 
 def project_kernel(
@@ -223,7 +224,7 @@
     def fetch(n):
         return pltpu.make_async_copy(w_ref.at[:, pl.ds(n * TILE_N, TILE_N)], tiles_ref.at[n], sems.at[n])
 
-    for n in range(tiles):
+    for n in range(AHEAD):
         fetch(n).start()
     for head in range(HEADS):
         for core in range(2):
@@ -234,6 +235,8 @@
     square = 0.0
     for n in range(tiles):
         fetch(n).wait()
+        if n + AHEAD < tiles:
+            fetch(n + AHEAD).start()
         part = jnp.dot(rows_ref[...], tiles_ref[n], preferred_element_type=jnp.float32)
         proj_ref[n] = part
         part_sum = jnp.sum(part, axis=1, keepdims=True)
@@ -246,11 +249,13 @@
     inverse = 1.0 / jnp.sqrt(variance + 1e-06)
 
     def reduce(n, patches):
-        at = pl.ds(pl.multiple_of(n * TILE_N, TILE_N), TILE_N)
+        at = slice(n * TILE_N, (n + 1) * TILE_N)
         normed = (proj_ref[n] - mean) * inverse * (1.0 + scale_ref[:, at]) + shift_ref[:, at]
         return patches + jnp.dot(normed.astype(jnp.bfloat16), final_ref[at, :], preferred_element_type=jnp.float32)
 
-    patches = lax.fori_loop(0, tiles, reduce, jnp.zeros((PH * WIDE, 4 * C_LAT), jnp.float32), unroll=2)
+    patches = jnp.zeros((PH * WIDE, 4 * C_LAT), jnp.float32)
+    for n in range(tiles):
+        patches = reduce(n, patches)
     place = lax.broadcasted_iota(jnp.int32, patches.shape, 0) // PH + (band_ref[0] * BAND - 1)
     patches = jnp.where((place >= 0) & (place < PW), patches, 0.0).astype(jnp.bfloat16)
     wide = 0.0
@@ -280,33 +285,43 @@
     )(band, gathered, w_out, shift_vec.reshape(1, D), scale_vec.reshape(1, D), w_final, choose, order)
 
 
-def conv_kernel(frame_ref, now_ref, one_ref, two_ref, w_ref, out_ref, taps_ref, spread_ref):
+def windows_of(grid, odd):
     rows = BAND * PH
-    taps_ref[...] = jnp.zeros_like(taps_ref)
+    row = lax.rem(lax.broadcasted_iota(jnp.int32, (rows, 128), 0), PH)
+    if odd == 0:
+        beside = jnp.where(row == 0, 0.0, pltpu.roll(grid, 1, 0))
+    else:
+        beside = jnp.where(row == PH - 1, 0.0, pltpu.roll(grid, rows - 1, 0))
+    return jnp.concatenate([grid, beside], axis=1).astype(jnp.bfloat16)
+
+
+def conv_now_kernel(now_ref, w_ref, part_ref, taps_ref, last_ref):
+    for taps, frames in ((taps_ref, (0, 1)), (last_ref, (2,))):
+        taps[...] = jnp.zeros_like(taps)
+        for odd in range(2):
+            for n, a in enumerate(frames):
+                for b in range(3):
+                    y = odd + b - 1
+                    offset = {-1: 192, 0: 0, 1: 64, 2: 128}[y]
+                    for j in range(2):
+                        for e in range(3):
+                            at = offset + (j + e) * C_LAT
+                            tap = ((a * 3 + b) * 3 + e) * C_LAT
+                            taps[odd, n, at : at + C_LAT, j * C_VAE : (j + 1) * C_VAE] = w_ref[tap : tap + C_LAT, :]
+    now = now_ref[...].astype(jnp.float32)
     for odd in range(2):
-        for a in range(3):
-            for b in range(3):
-                y = odd + b - 1
-                offset = {-1: 192, 0: 0, 1: 64, 2: 128}[y]
-                for j in range(2):
-                    for e in range(3):
-                        at = offset + (j + e) * C_LAT
-                        tap = ((a * 3 + b) * 3 + e) * C_LAT
-                        taps_ref[odd, a, at : at + C_LAT, j * C_VAE : (j + 1) * C_VAE] = w_ref[tap : tap + C_LAT, :]
+        part_ref[odd] = jnp.dot(windows_of(now, odd), last_ref[odd, 0], preferred_element_type=jnp.float32)
+
+
+def conv_kernel(frame_ref, now_ref, one_ref, two_ref, part_ref, taps_ref, out_ref, spread_ref):
     frame = frame_ref[0]
     now = now_ref[...].astype(jnp.float32)
     one = jnp.where(frame >= 1, one_ref[...].astype(jnp.float32), now)
     two = jnp.where(frame >= 2, two_ref[...].astype(jnp.float32), one)
-    row = lax.rem(lax.broadcasted_iota(jnp.int32, (rows, 128), 0), PH)
     for odd in range(2):
-        result = jnp.zeros((rows, 2 * C_VAE), jnp.float32)
-        for a, grid in enumerate((two, one, now)):
-            if odd == 0:
-                beside = jnp.where(row == 0, 0.0, pltpu.roll(grid, 1, 0))
-            else:
-                beside = jnp.where(row == PH - 1, 0.0, pltpu.roll(grid, rows - 1, 0))
-            window = jnp.concatenate([grid, beside], axis=1).astype(jnp.bfloat16)
-            result = result + jnp.dot(window, taps_ref[odd, a], preferred_element_type=jnp.float32)
+        result = part_ref[odd]
+        for a, grid in enumerate((two, one)):
+            result = result + jnp.dot(windows_of(grid, odd), taps_ref[odd, a], preferred_element_type=jnp.float32)
         for col in range(BAND):
             for j in range(2):
                 for part in range(C_VAE // 128):
@@ -320,20 +335,30 @@
 
 
 def convolve(frame, now, one, two, w_conv):
+    rows = BAND * PH
+    vmem = pl.BlockSpec(memory_space=pltpu.VMEM)
+    taps = w_conv.reshape(27 * C_LAT, C_VAE)
+    part, taps = pl.pallas_call(
+        conv_now_kernel,
+        in_specs=[vmem] * 2,
+        out_specs=[vmem] * 2,
+        out_shape=[
+            jax.ShapeDtypeStruct((2, rows, 2 * C_VAE), jnp.float32),
+            jax.ShapeDtypeStruct((2, 2, 256, 2 * C_VAE), jnp.bfloat16),
+        ],
+        scratch_shapes=[pltpu.VMEM((2, 1, 256, 2 * C_VAE), jnp.bfloat16)],
+        compiler_params=pltpu.CompilerParams(vmem_limit_bytes=24 * MIB),
+        cost_estimate=pl.CostEstimate(flops=rows * 2 ** 20, bytes_accessed=2 ** 22, transcendentals=0),
+    )(now, taps)
     return pl.pallas_call(
         conv_kernel,
         grid=(1,),
-        in_specs=[pl.BlockSpec(memory_space=pltpu.SMEM)]
-        + [pl.BlockSpec((BAND * PH, 128), lambda i: (0, 0))] * 3
-        + [pl.BlockSpec((27 * C_LAT, C_VAE), lambda i: (0, 0))],
+        in_specs=[pl.BlockSpec(memory_space=pltpu.SMEM)] + [vmem] * 5,
         out_specs=pl.BlockSpec((2 * BAND, 2 * PH, C_VAE), lambda i: (0, 0, 0)),
         out_shape=jax.ShapeDtypeStruct((2 * BAND, 2 * PH, C_VAE), jnp.bfloat16),
-        scratch_shapes=[
-            pltpu.VMEM((2, 3, 256, 2 * C_VAE), jnp.bfloat16),
-            pltpu.VMEM((C_VAE // 128, 4 * BAND * PH, 128), jnp.float32),
-        ],
+        scratch_shapes=[pltpu.VMEM((C_VAE // 128, 4 * BAND * PH, 128), jnp.float32)],
         compiler_params=pltpu.CompilerParams(vmem_limit_bytes=24 * MIB),
-    )(frame, now, one, two, w_conv.reshape(27 * C_LAT, C_VAE))
+    )(frame, now, one, two, part, taps)
 
 
 def ring(x, axis, by):

time: 145 us -> 144 us (level)
  transfers between devices with their start and end apart: 11 -> 11, of which waited for: 2 -> 2; matrix products, arithmetic and copies ran while one was open for 0% -> 0% of each run, Pallas kernels for 28% -> 29%
where the time goes in v3:
time: 144 us
  Pallas kernels  57.7 us (40%)
  blocking collectives  33.3 us (23%)
  starting transfers between devices  32.2 us (22%)
  waiting for transfers between devices  16.7 us (12%)
  local copies, waits for them, and re-layouts  3.13 us (2%)
    pallas_call x6, Pallas kernels, attend(): pl.pallas_call(functools.partial(attention_kernel, pieces=len(kvs), first...  46.7 us
    all_to_all x1, blocking collectives, per_device(): lax.all_to_all(outgoing, PLANE, 0, 0, tiled=True)  33.3 us
    ppermute x8, starting transfers between devices, ring(): return lax.ppermute(x, axis, [(i, (i + by) % count) for i in range(count)])  19.9 us
    all_to_all x1, waiting for transfers between devices, per_device(): gathered = lax.all_to_all(banded, ('zl', 'x', 'zh', 'c'), 0, 0, tiled=True)  14.4 us
    pallas_call x1, Pallas kernels, project(): pl.pallas_call(project_kernel, in_specs=[pl.BlockSpec(memory_space=pltpu....  7.19 us
    ppermute x2, starting transfers between devices, later(): lax.ppermute(x, ('y', 'zl'), [(i, i + by) for i in range(count - by)])  7.09 us
    all_to_all x1, starting transfers between devices, per_device(): gathered = lax.all_to_all(banded, ('zl', 'x', 'zh', 'c'), 0, 0, tiled=True)  5.28 us
  transfers between devices with their start and end apart: 11, of which 2 were waited for; matrix products, arithmetic and copies ran while one was open for 0% of the time, Pallas kernels for 29%

profile of v3, /device:TPU:40, one launch (start us, length us, event | category | flops | bytes accessed | tf_op | source)
XLA Modules:
  0.0 143.7 jit_solution(17542945163258974061)
XLA Ops:
  0.0 0.0 copy-start
  0.0 1.3 bitcast_bitcast_fusion.2
  1.3 0.0 copy-done
  1.3 1.3 bitcast_bitcast_fusion
  2.6 0.3 pad_maximum_fusion
  2.9 33.3 %all_to_all.10 = bf16[16,160,384]{2,1,0:T(8,128)(2,1)S(1)} all-to-all(bf16[16,160,384]{2,1,0:T(8,128)(2,1)S(1)} %pad_maximum_fusion), channel_id=1, replica_groups=mesh['y'=4,'zl'=2,'x'=4,'zh'=2,'c'=2] {'zl','x','zh'}, dimensions={0} | all-to-all | bytes 3932160 | tf_op jit(solution)/shard_map/all_to_all | solution.py:381
  36.2 0.1 collective-permute-start.2
  36.3 0.1 fusion
  36.4 1.6 %collective-permute-start = (bf16[1280,256]{1,0:T(8,128)(2,1)S(1)}, bf16[1280,256]{1,0:T(8,128)(2,1)S(1)}, u32[]{:S(2)}, u32[]{:S(2)}) collective-permute-start(bf16[1280,256]{1,0:T(8,128)(2,1)S(1)} %get-tuple-element.21.refs_1_), channel_id=1, source_target_pairs={{0,32},{32,64},{64,96},{96,0},{1,33},{33,65},{65,97},{97,1},{2,34}... | collective-permute-start | bytes 1966088 | tf_op jit(solution)/shard_map/ppermute | solution.py:366
  38.0 0.5 collective-permute-start.1
  38.5 5.9 %shard_map.109.refs_3_ = f32[144,5120]{1,0:T(8,128)S(1)} custom-call(bf16[2560,128]{1,0:T(8,128)(2,1)S(1)} %slice.15.refs_0_, bf16[1280,256]{1,0:T(8,128)(2,1)S(1)} %get-tuple-element.21.refs_1_, bf16[1280,256]{1,0:T(8,128)(2,1)S(1)} %get-tuple-element.22.refs_2_), custom_call_target="tpu_custom_call" | custom-call | flops 5033164800 | bytes 4915200 | tf_op jit(solution)/shard_map/pallas_call | solution.py:130
  44.4 0.0 collective-permute-done.2.refs_0_
  44.5 14.4 %collective-permute-start.5 = (bf16[1280,256]{1,0:T(8,128)(2,1)S(1)}, bf16[1280,256]{1,0:T(8,128)(2,1)S(1)}, u32[]{:S(2)}, u32[]{:S(2)}) collective-permute-start(bf16[1280,256]{1,0:T(8,128)(2,1)S(1)} %get-tuple-element.22.refs_2_), channel_id=1, source_target_pairs={{0,32},{32,64},{64,96},{96,0},{1,33},{33,65},{65,97},{97,1},{2,34}... | collective-permute-start | bytes 1966088 | tf_op jit(solution)/shard_map/ppermute | solution.py:366
  58.9 0.0 collective-permute-start.6
  58.9 5.9 %shard_map.110.refs_3_ = f32[144,5120]{1,0:T(8,128)S(1)} custom-call(bf16[2560,128]{1,0:T(8,128)(2,1)S(1)} %collective-permute-done.2.refs_0_, bf16[1280,256]{1,0:T(8,128)(2,1)S(1)} %get-tuple-element.21.refs_1_, bf16[1280,256]{1,0:T(8,128)(2,1)S(1)} %get-tuple-element.22.refs_2_, f32[144,5120]{1,0:T(8,128)S(1)} %shard_map.109.refs_3_), custom_call_target="tpu_custom_call", output_to_operand_aliasing={{}: (3, {})} | custom-call | flops 5033164800 | bytes 4915200 | tf_op jit(solution)/shard_map/pallas_call | solution.py:130
  64.8 0.1 pad_maximum_fusion.1.refs_0_
  64.9 0.0 collective-permute-done.refs_1_
  64.9 0.0 collective-permute-done.1.refs_2_
  64.9 2.1 %collective-permute-start.3 = (bf16[1280,256]{1,0:T(8,128)(2,1)S(1)}, bf16[1280,256]{1,0:T(8,128)(2,1)S(1)}, u32[]{:S(2)}, u32[]{:S(2)}) collective-permute-start(bf16[1280,256]{1,0:T(8,128)(2,1)S(1)} %collective-permute-done.refs_1_), channel_id=1, source_target_pairs={{0,32},{32,64},{64,96},{96,0},{1,33},{33,65},{65,97},{97,1},{2,34}... | collective-permute-start | bytes 1966088 | tf_op jit(solution)/shard_map/ppermute | solution.py:366
  67.0 0.2 collective-permute-start.4
  67.2 11.6 %shard_map.111.refs_3_ = f32[144,5120]{1,0:T(8,128)S(1)} custom-call(bf16[5120,128]{1,0:T(8,128)(2,1)S(1)} %pad_maximum_fusion.1.refs_0_, bf16[1280,256]{1,0:T(8,128)(2,1)S(1)} %collective-permute-done.refs_1_, bf16[1280,256]{1,0:T(8,128)(2,1)S(1)} %collective-permute-done.1.refs_2_, f32[144,5120]{1,0:T(8,128)S(1)} %shard_map.110.refs_3_), custom_call_target="tpu_custom_call" | custom-call | flops 10066329600 | bytes 8519680 | tf_op jit(solution)/shard_map/pallas_call | solution.py:130
  78.8 0.0 collective-permute-done.5.refs_1_
  78.9 0.0 collective-permute-done.6.refs_2_
  78.9 11.6 %shard_map.112.refs_3_ = f32[144,5120]{1,0:T(8,128)S(1)} custom-call(bf16[5120,128]{1,0:T(8,128)(2,1)S(1)} %pad_maximum_fusion.1.refs_0_, bf16[1280,256]{1,0:T(8,128)(2,1)S(1)} %collective-permute-done.5.refs_1_, bf16[1280,256]{1,0:T(8,128)(2,1)S(1)} %collective-permute-done.6.refs_2_, f32[144,5120]{1,0:T(8,128)S(1)} %shard_map.111.refs_3_), custom_call_target="tpu_custom_call" | custom-call | flops 10066329600 | bytes 8519680 | tf_op jit(solution)/shard_map/pallas_call | solution.py:130
  90.5 0.0 collective-permute-done.3.refs_1_
  90.5 0.0 collective-permute-done.4.refs_2_
  90.5 5.8 %shard_map.114 = f32[144,2560]{1,0:T(8,128)S(1)} custom-call(bf16[2560,128]{1,0:T(8,128)(2,1)S(1)} %collective-permute-done.2.refs_0_, bf16[1280,256]{1,0:T(8,128)(2,1)S(1)} %collective-permute-done.3.refs_1_, bf16[1280,256]{1,0:T(8,128)(2,1)S(1)} %collective-permute-done.4.refs_2_, f32[144,5120]{1,0:T(8,128)S(1)} %shard_map.112.refs_3_), custom_call_target="tpu_custom_call" | custom-call | flops 5033164800 | bytes 4915200 | tf_op jit(solution)/shard_map/pallas_call | solution.py:130
  96.3 0.0 copy-start.1
  96.4 1.0 collective-permute-start.7
  97.3 5.8 %shard_map.113.mine_ref = f32[144,2560]{1,0:T(8,128)S(1)} custom-call(bf16[2560,128]{1,0:T(8,128)(2,1)S(1)} %slice.15.refs_0_, bf16[1280,256]{1,0:T(8,128)(2,1)S(1)} %collective-permute-done.3.refs_1_, bf16[1280,256]{1,0:T(8,128)(2,1)S(1)} %collective-permute-done.4.refs_2_, f32[144,5120]{1,0:T(8,128)S(1)} %shard_map.112.refs_3_), custom_call_target="tpu_custom_call" | custom-call | flops 5033164800 | bytes 4915200 | tf_op jit(solution)/shard_map/pallas_call | solution.py:130
  103.1 0.0 collective-permute-done.7.other_ref
  103.1 0.0 copy-done.1
  103.1 1.9 %shard_map.115 = bf16[32,112,128]{2,1,0:T(8,128)(2,1)} custom-call(f32[144,2560]{1,0:T(8,128)S(1)} %shard_map.113.mine_ref, f32[144,2560]{1,0:T(8,128)S(1)} %collective-permute-done.7.other_ref, bf16[896,640]{1,0:T(8,128)(2,1)S(1)} %copy-done.1), custom_call_target="tpu_custom_call" | custom-call | tf_op jit(solution)/shard_map/pallas_call | solution.py:189
  105.1 0.0 copy-start.5
  105.1 5.3 %all-to-all-start.1 = ((bf16[32,112,128]{2,1,0:T(8,128)(2,1)}), bf16[32,112,128]{2,1,0:T(8,128)(2,1)S(1)}, u32[]{:S(2)}, u32[]{:S(2)}) async-start(bf16[32,112,128]{2,1,0:T(8,128)(2,1)} %shard_map.115), calls=%async_computation.1 | async-start | bytes 1835008 | tf_op jit(solution)/shard_map/all_to_all | solution.py:404
  110.4 0.4 copy.16.final_ref
  110.8 14.4 %all-to-all-done.1 = bf16[32,112,128]{2,1,0:T(8,128)(2,1)S(1)} async-done(((bf16[32,112,128]{2,1,0:T(8,128)(2,1)}), bf16[32,112,128]{2,1,0:T(8,128)(2,1)S(1)}, u32[]{:S(2)}, u32[]{:S(2)}) %all-to-all-start.1) | async-done | bytes 917536 | tf_op jit(solution)/shard_map/all_to_all | solution.py:404
  125.2 0.0 copy-done.2
  125.2 0.0 copy-done.4
  125.2 0.0 copy-start.6
  125.2 7.2 %shard_map.116.now_ref = bf16[160,128]{1,0:T(8,128)(2,1)S(1)} custom-call(s32[1]{0:T(128)} %bitcast.1.band_ref, bf16[16,2,112,128]{3,2,1,0:T(8,128)(2,1)S(1)} %bitcast.31, bf16[2048,3072]{1,0:T(8,128)(2,1)} %w_ref.1, f32[1,3072]{1,0:T(1,128)S(1)} %bitcast.32, f32[1,3072]{1,0:T(1,128)S(1)} %bitcast.33, bf16[3072,64]{1,0:T(8,128)(2,1)S(1)} %copy.16.final_ref, ...), custom_call_target="tpu_custom_call" | custom-call | tf_op jit(solution)/shard_map/pallas_call | solution.py:273
  132.4 3.9 %collective-permute-start.8 = (bf16[160,128]{1,0:T(8,128)(2,1)S(1)}, bf16[160,128]{1,0:T(8,128)(2,1)S(1)}, u32[]{:S(2)}, u32[]{:S(2)}) collective-permute-start(bf16[160,128]{1,0:T(8,128)(2,1)S(1)} %shard_map.116.now_ref), channel_id=1, source_target_pairs={{0,16},{16,32},{32,48},{48,64},{64,80},{80,96},{96,112},{1,17},{17... | collective-permute-start | bytes 122888 | tf_op jit(solution)/shard_map/ppermute | solution.py:371
  136.3 3.2 %collective-permute-start.9 = (bf16[160,128]{1,0:T(8,128)(2,1)S(1)}, bf16[160,128]{1,0:T(8,128)(2,1)S(1)}, u32[]{:S(2)}, u32[]{:S(2)}) collective-permute-start(bf16[160,128]{1,0:T(8,128)(2,1)S(1)} %shard_map.116.now_ref), channel_id=1, source_target_pairs={{0,32},{16,48},{32,64},{48,80},{64,96},{80,112},{1,33},{17,49},{33... | collective-permute-start | bytes 122888 | tf_op jit(solution)/shard_map/ppermute | solution.py:371
  139.5 0.0 copy-done.6
  139.5 0.4 shard_map.117
  140.0 0.0 collective-permute-done.8.one_ref
  140.0 2.2 %collective-permute-done.9.two_ref = bf16[160,128]{1,0:T(8,128)(2,1)S(1)} collective-permute-done((bf16[160,128]{1,0:T(8,128)(2,1)S(1)}, bf16[160,128]{1,0:T(8,128)(2,1)S(1)}, u32[]{:S(2)}, u32[]{:S(2)}) %collective-permute-start.9) | collective-permute-done | bytes 40992 | tf_op jit(solution)/shard_map/ppermute | solution.py:371
  142.2 1.5 %shard_map.118 = bf16[10,64,512]{2,1,0:T(8,128)(2,1)} custom-call(s32[1]{0:T(128)} %bitcast.frame_ref, bf16[160,128]{1,0:T(8,128)(2,1)S(1)} %shard_map.116.now_ref, bf16[160,128]{1,0:T(8,128)(2,1)S(1)} %collective-permute-done.8.one_ref, bf16[160,128]{1,0:T(8,128)(2,1)S(1)} %collective-permute-done.9.two_ref, ...), custom_call_target="tpu_custom_call" | custom-call | tf_op jit(solution)/shard_map/pallas_call | solution.py:353
  (8 shorter events, 0.1 us)
Async XLA Ops:
  0.0 1.3 copy-start
  36.2 8.2 %collective-permute-start.2 = (bf16[2560,128]{1,0:T(8,128)(2,1)S(1)}, bf16[2560,128]{1,0:T(8,128)(2,1)S(1)}, u32[]{:S(2)}, u32[]{:S(2)}) collective-permute-start(bf16[2560,128]{1,0:T(8,128)(2,1)S(1)} %slice.15.refs_0_), channel_id=1, source_target_pairs={{0,1},{1,0},{2,3},{3,2},{4,5},{5,4},{6,7},{7,6},{8,9},{9,8},{10,11... | collective-permute-start | bytes 1966088 | tf_op jit(solution)/shard_map/ppermute | solution.py:366
  36.4 28.5 %collective-permute-start = (bf16[1280,256]{1,0:T(8,128)(2,1)S(1)}, bf16[1280,256]{1,0:T(8,128)(2,1)S(1)}, u32[]{:S(2)}, u32[]{:S(2)}) collective-permute-start(bf16[1280,256]{1,0:T(8,128)(2,1)S(1)} %get-tuple-element.21.refs_1_), channel_id=1, source_target_pairs={{0,32},{32,64},{64,96},{96,0},{1,33},{33,65},{65,97},{97,1},{2,34}... | collective-permute-start | bytes 1966088 | tf_op jit(solution)/shard_map/ppermute | solution.py:366
  38.0 26.9 %collective-permute-start.1 = (bf16[1280,256]{1,0:T(8,128)(2,1)S(1)}, bf16[1280,256]{1,0:T(8,128)(2,1)S(1)}, u32[]{:S(2)}, u32[]{:S(2)}) collective-permute-start(bf16[1280,256]{1,0:T(8,128)(2,1)S(1)} %get-tuple-element.22.refs_2_), channel_id=1, source_target_pairs={{0,96},{32,0},{64,32},{96,64},{1,97},{33,1},{65,33},{97,65},{2,98}... | collective-permute-start | bytes 1966088 | tf_op jit(solution)/shard_map/ppermute | solution.py:366
  44.5 34.4 %collective-permute-start.5 = (bf16[1280,256]{1,0:T(8,128)(2,1)S(1)}, bf16[1280,256]{1,0:T(8,128)(2,1)S(1)}, u32[]{:S(2)}, u32[]{:S(2)}) collective-permute-start(bf16[1280,256]{1,0:T(8,128)(2,1)S(1)} %get-tuple-element.22.refs_2_), channel_id=1, source_target_pairs={{0,32},{32,64},{64,96},{96,0},{1,33},{33,65},{65,97},{97,1},{2,34}... | collective-permute-start | bytes 1966088 | tf_op jit(solution)/shard_map/ppermute | solution.py:366
  58.9 20.0 %collective-permute-start.6 = (bf16[1280,256]{1,0:T(8,128)(2,1)S(1)}, bf16[1280,256]{1,0:T(8,128)(2,1)S(1)}, u32[]{:S(2)}, u32[]{:S(2)}) collective-permute-start(bf16[1280,256]{1,0:T(8,128)(2,1)S(1)} %get-tuple-element.21.refs_1_), channel_id=1, source_target_pairs={{0,96},{32,0},{64,32},{96,64},{1,97},{33,1},{65,33},{97,65},{2,98}... | collective-permute-start | bytes 1966088 | tf_op jit(solution)/shard_map/ppermute | solution.py:366
  64.9 25.5 %collective-permute-start.3 = (bf16[1280,256]{1,0:T(8,128)(2,1)S(1)}, bf16[1280,256]{1,0:T(8,128)(2,1)S(1)}, u32[]{:S(2)}, u32[]{:S(2)}) collective-permute-start(bf16[1280,256]{1,0:T(8,128)(2,1)S(1)} %collective-permute-done.refs_1_), channel_id=1, source_target_pairs={{0,32},{32,64},{64,96},{96,0},{1,33},{33,65},{65,97},{97,1},{2,34}... | collective-permute-start | bytes 1966088 | tf_op jit(solution)/shard_map/ppermute | solution.py:366
  67.0 23.5 %collective-permute-start.4 = (bf16[1280,256]{1,0:T(8,128)(2,1)S(1)}, bf16[1280,256]{1,0:T(8,128)(2,1)S(1)}, u32[]{:S(2)}, u32[]{:S(2)}) collective-permute-start(bf16[1280,256]{1,0:T(8,128)(2,1)S(1)} %collective-permute-done.1.refs_2_), channel_id=1, source_target_pairs={{0,96},{32,0},{64,32},{96,64},{1,97},{33,1},{65,33},{97,65},{2,98}... | collective-permute-start | bytes 1966088 | tf_op jit(solution)/shard_map/ppermute | solution.py:366
  96.3 6.8 %copy-start.1 = (bf16[896,640]{1,0:T(8,128)(2,1)S(1)}, bf16[896,640]{1,0:T(8,128)(2,1)}, u32[]{:S(2)}) copy-start(bf16[896,640]{1,0:T(8,128)(2,1)} %constant.29.clone.choose_ref) | copy-start | bytes 3440644
  96.4 6.8 %collective-permute-start.7 = (f32[144,2560]{1,0:T(8,128)S(1)}, f32[144,2560]{1,0:T(8,128)S(1)}, u32[]{:S(2)}, u32[]{:S(2)}) collective-permute-start(f32[144,2560]{1,0:T(8,128)S(1)} %shard_map.114), channel_id=1, source_target_pairs={{0,1},{1,0},{2,3},{3,2},{4,5},{5,4},{6,7},{7,6},{8,9},{9,8},{10,11... | collective-permute-start | bytes 4423688 | tf_op jit(solution)/shard_map/ppermute | solution.py:366
  105.0 5.3 %copy-start.7 = (bf16[3072,64]{0,1:T(8,128)(2,1)S(1)}, bf16[3072,64]{0,1:T(8,128)(2,1)}, u32[]{:S(2)}) copy-start(bf16[3072,64]{0,1:T(8,128)(2,1)} %param.17) | copy-start | bytes 1179652
  105.1 20.1 %copy-start.2 = (bf16[160,160]{1,0:T(8,128)(2,1)S(1)}, bf16[160,160]{1,0:T(8,128)(2,1)}, u32[]{:S(2)}) copy-start(bf16[160,160]{1,0:T(8,128)(2,1)} %constant.31.clone.order_ref) | copy-start | bytes 153604
  105.1 20.1 %copy-start.3 = (bf16[3,64,128]{2,1,0:T(8,128)(2,1)S(1)}, bf16[3,64,128]{2,1,0:T(8,128)(2,1)}, u32[]{:S(2)}) copy-start(bf16[3,64,128]{2,1,0:T(8,128)(2,1)} %constant.30.clone.choose_ref) | copy-start | bytes 147460
  105.1 20.1 %copy-start.4 = (f32[3072]{0:T(1024)S(1)}, f32[3072]{0:T(1024)}, u32[]{:S(2)}) copy-start(f32[3072]{0:T(1024)} %param.15) | copy-start | bytes 36868
  105.1 20.1 %copy-start.5 = (f32[3072]{0:T(1024)S(1)}, f32[3072]{0:T(1024)}, u32[]{:S(2)}) copy-start(f32[3072]{0:T(1024)} %param.16) | copy-start | bytes 36868
  105.1 20.1 %all-to-all-start.1 = ((bf16[32,112,128]{2,1,0:T(8,128)(2,1)}), bf16[32,112,128]{2,1,0:T(8,128)(2,1)S(1)}, u32[]{:S(2)}, u32[]{:S(2)}) async-start(bf16[32,112,128]{2,1,0:T(8,128)(2,1)} %shard_map.115), calls=%async_computation.1 | async-start | bytes 1835008 | tf_op jit(solution)/shard_map/all_to_all | solution.py:404
  125.2 14.3 %copy-start.6 = (bf16[3,3,3,16,512]{4,3,2,1,0:T(8,128)(2,1)S(1)}, bf16[3,3,3,16,512]{4,3,2,1,0:T(8,128)(2,1)}, u32[]{:S(2)}) copy-start(bf16[3,3,3,16,512]{4,3,2,1,0:T(8,128)(2,1)} %param.18) | copy-start | bytes 1327108
  132.4 7.6 %collective-permute-start.8 = (bf16[160,128]{1,0:T(8,128)(2,1)S(1)}, bf16[160,128]{1,0:T(8,128)(2,1)S(1)}, u32[]{:S(2)}, u32[]{:S(2)}) collective-permute-start(bf16[160,128]{1,0:T(8,128)(2,1)S(1)} %shard_map.116.now_ref), channel_id=1, source_target_pairs={{0,16},{16,32},{32,48},{48,64},{64,80},{80,96},{96,112},{1,17},{17... | collective-permute-start | bytes 122888 | tf_op jit(solution)/shard_map/ppermute | solution.py:371
  136.3 5.9 %collective-permute-start.9 = (bf16[160,128]{1,0:T(8,128)(2,1)S(1)}, bf16[160,128]{1,0:T(8,128)(2,1)S(1)}, u32[]{:S(2)}, u32[]{:S(2)}) collective-permute-start(bf16[160,128]{1,0:T(8,128)(2,1)S(1)} %shard_map.116.now_ref), channel_id=1, source_target_pairs={{0,32},{16,48},{32,64},{48,80},{64,96},{80,112},{1,33},{17,49},{33... | collective-permute-start | bytes 122888 | tf_op jit(solution)/shard_map/ppermute | solution.py:371

commit v4 on v3

--- a/solution.py
+++ b/solution.py
@@ -164,30 +164,33 @@
 
 
 def combine_kernel(mine_ref, other_ref, choose_ref, out_ref):
-    for frame in range(2):
-        halves = []
-        for half in range(2):
-            at = slice((2 * frame + half) * ROWS, (2 * frame + half + 1) * ROWS)
-            ref_a, ref_b = (mine_ref[HD + 8 : HD + 9, at], other_ref[HD + 8 : HD + 9, at])
-            top = jnp.maximum(ref_a, ref_b)
-            gain_a, gain_b = (jnp.exp2(ref_a - top), jnp.exp2(ref_b - top))
-            total = jnp.sum(
-                mine_ref[HD : HD + 8, at] * gain_a + other_ref[HD : HD + 8, at] * gain_b,
-                axis=0,
-                keepdims=True,
-            )
-            attended = (mine_ref[0:HD, at] * gain_a + other_ref[0:HD, at] * gain_b) / total
-            halves.append(attended.astype(jnp.bfloat16))
-        banded = dot_nt(choose_ref[...], jnp.concatenate(halves, axis=0))
-        upper, lower = (banded[:, n * HD : (n + 1) * HD].reshape(BANDS, WIDE, 8, HD) for n in range(2))
-        rows = jnp.concatenate([upper, lower], axis=2).astype(jnp.bfloat16)
-        out_ref[frame * BANDS : (frame + 1) * BANDS] = rows.reshape(BANDS, WIDE * 16, HD)
+    frame = pl.program_id(0)
+    halves = []
+    for half in range(2):
+        at = pl.ds(pl.multiple_of((2 * frame + half) * ROWS, ROWS), ROWS)
+        ref_a, ref_b = (mine_ref[HD + 8 : HD + 9, at], other_ref[HD + 8 : HD + 9, at])
+        top = jnp.maximum(ref_a, ref_b)
+        gain_a, gain_b = (jnp.exp2(ref_a - top), jnp.exp2(ref_b - top))
+        total = jnp.sum(
+            mine_ref[HD : HD + 8, at] * gain_a + other_ref[HD : HD + 8, at] * gain_b,
+            axis=0,
+            keepdims=True,
+        )
+        attended = (mine_ref[0:HD, at] * gain_a + other_ref[0:HD, at] * gain_b) / total
+        halves.append(attended.astype(jnp.bfloat16))
+    banded = dot_nt(choose_ref[...], jnp.concatenate(halves, axis=0))
+    upper, lower = (banded[:, n * HD : (n + 1) * HD].reshape(BANDS, WIDE, 8, HD) for n in range(2))
+    rows = jnp.concatenate([upper, lower], axis=2).astype(jnp.bfloat16)
+    out_ref[...] = rows.reshape(BANDS, WIDE * 16, HD)
 
 
 def combine(mine, other):
     choose = jnp.asarray(band_selection(), jnp.bfloat16)
     return pl.pallas_call(
         combine_kernel,
+        grid=(2,),
+        in_specs=[pl.BlockSpec(memory_space=pltpu.VMEM)] * 3,
+        out_specs=pl.BlockSpec((BANDS, WIDE * 16, HD), lambda i: (i, 0, 0)),
         out_shape=jax.ShapeDtypeStruct((2 * BANDS, WIDE * 16, HD), jnp.bfloat16),
         compiler_params=pltpu.CompilerParams(vmem_limit_bytes=20 * MIB),
     )(mine, other, choose)
@@ -314,22 +317,25 @@
 
 
 def conv_kernel(frame_ref, now_ref, one_ref, two_ref, part_ref, taps_ref, out_ref, spread_ref):
+    width = out_ref.shape[2]
+    start = pl.program_id(0) * width
     frame = frame_ref[0]
     now = now_ref[...].astype(jnp.float32)
     one = jnp.where(frame >= 1, one_ref[...].astype(jnp.float32), now)
     two = jnp.where(frame >= 2, two_ref[...].astype(jnp.float32), one)
     for odd in range(2):
-        result = part_ref[odd]
-        for a, grid in enumerate((two, one)):
-            result = result + jnp.dot(windows_of(grid, odd), taps_ref[odd, a], preferred_element_type=jnp.float32)
-        for col in range(BAND):
-            for j in range(2):
-                for part in range(C_VAE // 128):
-                    at = j * C_VAE + part * 128
+        windows = [windows_of(grid, odd) for grid in (two, one)]
+        for j in range(2):
+            lanes = pl.ds(pl.multiple_of(j * C_VAE + start, width), width)
+            result = part_ref[odd, :, lanes]
+            for a in range(2):
+                result = result + jnp.dot(windows[a], taps_ref[odd, a, :, lanes], preferred_element_type=jnp.float32)
+            for col in range(BAND):
+                for part in range(width // 128):
                     spread_ref[part, pl.ds((2 * col + j) * 2 * PH + odd, PH, stride=2), :] = result[
-                        col * PH : (col + 1) * PH, at : at + 128
+                        col * PH : (col + 1) * PH, part * 128 : (part + 1) * 128
                     ]
-    for part in range(C_VAE // 128):
+    for part in range(width // 128):
         final = spread_ref[part].reshape(2 * BAND, 2 * PH, 128)
         out_ref[:, :, part * 128 : (part + 1) * 128] = final.astype(jnp.bfloat16)
 
@@ -352,11 +358,11 @@
     )(now, taps)
     return pl.pallas_call(
         conv_kernel,
-        grid=(1,),
+        grid=(2,),
         in_specs=[pl.BlockSpec(memory_space=pltpu.SMEM)] + [vmem] * 5,
-        out_specs=pl.BlockSpec((2 * BAND, 2 * PH, C_VAE), lambda i: (0, 0, 0)),
+        out_specs=pl.BlockSpec((2 * BAND, 2 * PH, C_VAE // 2), lambda i: (0, 0, i)),
         out_shape=jax.ShapeDtypeStruct((2 * BAND, 2 * PH, C_VAE), jnp.bfloat16),
-        scratch_shapes=[pltpu.VMEM((C_VAE // 128, 4 * BAND * PH, 128), jnp.float32)],
+        scratch_shapes=[pltpu.VMEM((C_VAE // 256, 4 * BAND * PH, 128), jnp.float32)],
         compiler_params=pltpu.CompilerParams(vmem_limit_bytes=24 * MIB),
     )(frame, now, one, two, part, taps)
 

time: 144 us -> 144 us (level)
  no operation moved by 1% of the time
where the time goes in v4:
time: 144 us
  Pallas kernels  57.9 us (40%)
  blocking collectives  33.3 us (23%)
  starting transfers between devices  32.2 us (22%)
  waiting for transfers between devices  16.7 us (12%)
  local copies, waits for them, and re-layouts  3.13 us (2%)
    pallas_call x6, Pallas kernels, attend(): pl.pallas_call(functools.partial(attention_kernel, pieces=len(kvs), first...  46.7 us
    all_to_all x1, blocking collectives, per_device(): lax.all_to_all(outgoing, PLANE, 0, 0, tiled=True)  33.3 us
    ppermute x8, starting transfers between devices, ring(): return lax.ppermute(x, axis, [(i, (i + by) % count) for i in range(count)])  19.9 us
    all_to_all x1, waiting for transfers between devices, per_device(): gathered = lax.all_to_all(banded, ('zl', 'x', 'zh', 'c'), 0, 0, tiled=True)  14.4 us
    pallas_call x1, Pallas kernels, project(): pl.pallas_call(project_kernel, in_specs=[pl.BlockSpec(memory_space=pltpu....  7.19 us
    ppermute x2, starting transfers between devices, later(): lax.ppermute(x, ('y', 'zl'), [(i, i + by) for i in range(count - by)])  7.09 us
    all_to_all x1, starting transfers between devices, per_device(): gathered = lax.all_to_all(banded, ('zl', 'x', 'zh', 'c'), 0, 0, tiled=True)  5.28 us
  transfers between devices with their start and end apart: 11, of which 2 were waited for; matrix products, arithmetic and copies ran while one was open for 0% of the time, Pallas kernels for 29%

profile of v4, /device:TPU:40, one launch (start us, length us, event | category | flops | bytes accessed | tf_op | source)
XLA Modules:
  0.0 143.9 jit_solution(17299914808559576065)
XLA Ops:
  0.0 0.0 copy-start
  0.0 1.3 bitcast_bitcast_fusion.2
  1.3 0.0 copy-done
  1.3 1.3 bitcast_bitcast_fusion
  2.6 0.3 pad_maximum_fusion
  2.9 33.3 %all_to_all.10 = bf16[16,160,384]{2,1,0:T(8,128)(2,1)S(1)} all-to-all(bf16[16,160,384]{2,1,0:T(8,128)(2,1)S(1)} %pad_maximum_fusion), channel_id=1, replica_groups=mesh['y'=4,'zl'=2,'x'=4,'zh'=2,'c'=2] {'zl','x','zh'}, dimensions={0} | all-to-all | bytes 3932160 | tf_op jit(solution)/shard_map/all_to_all | solution.py:387
  36.2 0.1 collective-permute-start.2
  36.3 0.1 fusion
  36.4 1.6 %collective-permute-start = (bf16[1280,256]{1,0:T(8,128)(2,1)S(1)}, bf16[1280,256]{1,0:T(8,128)(2,1)S(1)}, u32[]{:S(2)}, u32[]{:S(2)}) collective-permute-start(bf16[1280,256]{1,0:T(8,128)(2,1)S(1)} %get-tuple-element.21.refs_1_), channel_id=1, source_target_pairs={{0,32},{32,64},{64,96},{96,0},{1,33},{33,65},{65,97},{97,1},{2,34}... | collective-permute-start | bytes 1966088 | tf_op jit(solution)/shard_map/ppermute | solution.py:372
  38.0 0.5 collective-permute-start.1
  38.5 5.9 %shard_map.109.refs_3_ = f32[144,5120]{1,0:T(8,128)S(1)} custom-call(bf16[2560,128]{1,0:T(8,128)(2,1)S(1)} %slice.15.refs_0_, bf16[1280,256]{1,0:T(8,128)(2,1)S(1)} %get-tuple-element.21.refs_1_, bf16[1280,256]{1,0:T(8,128)(2,1)S(1)} %get-tuple-element.22.refs_2_), custom_call_target="tpu_custom_call" | custom-call | flops 5033164800 | bytes 4915200 | tf_op jit(solution)/shard_map/pallas_call | solution.py:130
  44.4 0.0 collective-permute-done.2.refs_0_
  44.5 14.4 %collective-permute-start.5 = (bf16[1280,256]{1,0:T(8,128)(2,1)S(1)}, bf16[1280,256]{1,0:T(8,128)(2,1)S(1)}, u32[]{:S(2)}, u32[]{:S(2)}) collective-permute-start(bf16[1280,256]{1,0:T(8,128)(2,1)S(1)} %get-tuple-element.22.refs_2_), channel_id=1, source_target_pairs={{0,32},{32,64},{64,96},{96,0},{1,33},{33,65},{65,97},{97,1},{2,34}... | collective-permute-start | bytes 1966088 | tf_op jit(solution)/shard_map/ppermute | solution.py:372
  58.9 0.0 collective-permute-start.6
  58.9 5.9 %shard_map.110.refs_3_ = f32[144,5120]{1,0:T(8,128)S(1)} custom-call(bf16[2560,128]{1,0:T(8,128)(2,1)S(1)} %collective-permute-done.2.refs_0_, bf16[1280,256]{1,0:T(8,128)(2,1)S(1)} %get-tuple-element.21.refs_1_, bf16[1280,256]{1,0:T(8,128)(2,1)S(1)} %get-tuple-element.22.refs_2_, f32[144,5120]{1,0:T(8,128)S(1)} %shard_map.109.refs_3_), custom_call_target="tpu_custom_call", output_to_operand_aliasing={{}: (3, {})} | custom-call | flops 5033164800 | bytes 4915200 | tf_op jit(solution)/shard_map/pallas_call | solution.py:130
  64.8 0.1 pad_maximum_fusion.1.refs_0_
  64.9 0.0 collective-permute-done.refs_1_
  64.9 0.0 collective-permute-done.1.refs_2_
  64.9 2.1 %collective-permute-start.3 = (bf16[1280,256]{1,0:T(8,128)(2,1)S(1)}, bf16[1280,256]{1,0:T(8,128)(2,1)S(1)}, u32[]{:S(2)}, u32[]{:S(2)}) collective-permute-start(bf16[1280,256]{1,0:T(8,128)(2,1)S(1)} %collective-permute-done.refs_1_), channel_id=1, source_target_pairs={{0,32},{32,64},{64,96},{96,0},{1,33},{33,65},{65,97},{97,1},{2,34}... | collective-permute-start | bytes 1966088 | tf_op jit(solution)/shard_map/ppermute | solution.py:372
  67.0 0.2 collective-permute-start.4
  67.2 11.6 %shard_map.111.refs_3_ = f32[144,5120]{1,0:T(8,128)S(1)} custom-call(bf16[5120,128]{1,0:T(8,128)(2,1)S(1)} %pad_maximum_fusion.1.refs_0_, bf16[1280,256]{1,0:T(8,128)(2,1)S(1)} %collective-permute-done.refs_1_, bf16[1280,256]{1,0:T(8,128)(2,1)S(1)} %collective-permute-done.1.refs_2_, f32[144,5120]{1,0:T(8,128)S(1)} %shard_map.110.refs_3_), custom_call_target="tpu_custom_call" | custom-call | flops 10066329600 | bytes 8519680 | tf_op jit(solution)/shard_map/pallas_call | solution.py:130
  78.8 0.0 collective-permute-done.5.refs_1_
  78.9 0.0 collective-permute-done.6.refs_2_
  78.9 11.6 %shard_map.112.refs_3_ = f32[144,5120]{1,0:T(8,128)S(1)} custom-call(bf16[5120,128]{1,0:T(8,128)(2,1)S(1)} %pad_maximum_fusion.1.refs_0_, bf16[1280,256]{1,0:T(8,128)(2,1)S(1)} %collective-permute-done.5.refs_1_, bf16[1280,256]{1,0:T(8,128)(2,1)S(1)} %collective-permute-done.6.refs_2_, f32[144,5120]{1,0:T(8,128)S(1)} %shard_map.111.refs_3_), custom_call_target="tpu_custom_call" | custom-call | flops 10066329600 | bytes 8519680 | tf_op jit(solution)/shard_map/pallas_call | solution.py:130
  90.5 0.0 collective-permute-done.3.refs_1_
  90.5 0.0 collective-permute-done.4.refs_2_
  90.5 5.8 %shard_map.114 = f32[144,2560]{1,0:T(8,128)S(1)} custom-call(bf16[2560,128]{1,0:T(8,128)(2,1)S(1)} %collective-permute-done.2.refs_0_, bf16[1280,256]{1,0:T(8,128)(2,1)S(1)} %collective-permute-done.3.refs_1_, bf16[1280,256]{1,0:T(8,128)(2,1)S(1)} %collective-permute-done.4.refs_2_, f32[144,5120]{1,0:T(8,128)S(1)} %shard_map.112.refs_3_), custom_call_target="tpu_custom_call" | custom-call | flops 5033164800 | bytes 4915200 | tf_op jit(solution)/shard_map/pallas_call | solution.py:130
  96.3 0.0 copy-start.1
  96.4 1.0 collective-permute-start.7
  97.3 5.8 %shard_map.113.mine_ref = f32[144,2560]{1,0:T(8,128)S(1)} custom-call(bf16[2560,128]{1,0:T(8,128)(2,1)S(1)} %slice.15.refs_0_, bf16[1280,256]{1,0:T(8,128)(2,1)S(1)} %collective-permute-done.3.refs_1_, bf16[1280,256]{1,0:T(8,128)(2,1)S(1)} %collective-permute-done.4.refs_2_, f32[144,5120]{1,0:T(8,128)S(1)} %shard_map.112.refs_3_), custom_call_target="tpu_custom_call" | custom-call | flops 5033164800 | bytes 4915200 | tf_op jit(solution)/shard_map/pallas_call | solution.py:130
  103.1 0.0 collective-permute-done.7.other_ref
  103.1 0.0 copy-done.1
  103.1 2.1 %shard_map.115 = bf16[32,112,128]{2,1,0:T(8,128)(2,1)} custom-call(f32[144,2560]{1,0:T(8,128)S(1)} %shard_map.113.mine_ref, f32[144,2560]{1,0:T(8,128)S(1)} %collective-permute-done.7.other_ref, bf16[896,640]{1,0:T(8,128)(2,1)S(1)} %copy-done.1), custom_call_target="tpu_custom_call" | custom-call | tf_op jit(solution)/shard_map/pallas_call | solution.py:189
  105.2 0.0 copy-start.5
  105.2 5.3 %all-to-all-start.1 = ((bf16[32,112,128]{2,1,0:T(8,128)(2,1)}), bf16[32,112,128]{2,1,0:T(8,128)(2,1)S(1)}, u32[]{:S(2)}, u32[]{:S(2)}) async-start(bf16[32,112,128]{2,1,0:T(8,128)(2,1)} %shard_map.115), calls=%async_computation.1 | async-start | bytes 1835008 | tf_op jit(solution)/shard_map/all_to_all | solution.py:410
  110.5 0.0 copy-done.7
  110.5 0.4 copy.16.final_ref
  110.9 14.4 %all-to-all-done.1 = bf16[32,112,128]{2,1,0:T(8,128)(2,1)S(1)} async-done(((bf16[32,112,128]{2,1,0:T(8,128)(2,1)}), bf16[32,112,128]{2,1,0:T(8,128)(2,1)S(1)}, u32[]{:S(2)}, u32[]{:S(2)}) %all-to-all-start.1) | async-done | bytes 917536 | tf_op jit(solution)/shard_map/all_to_all | solution.py:410
  125.3 0.0 copy-done.2
  125.3 0.0 copy-done.3
  125.4 0.0 copy-start.6
  125.4 7.2 %shard_map.116.now_ref = bf16[160,128]{1,0:T(8,128)(2,1)S(1)} custom-call(s32[1]{0:T(128)} %bitcast.1.band_ref, bf16[16,2,112,128]{3,2,1,0:T(8,128)(2,1)S(1)} %bitcast.31, bf16[2048,3072]{1,0:T(8,128)(2,1)} %w_ref.1, f32[1,3072]{1,0:T(1,128)S(1)} %bitcast.32, f32[1,3072]{1,0:T(1,128)S(1)} %bitcast.33, bf16[3072,64]{1,0:T(8,128)(2,1)S(1)} %copy.16.final_ref, ...), custom_call_target="tpu_custom_call" | custom-call | tf_op jit(solution)/shard_map/pallas_call | solution.py:276
  132.6 3.9 %collective-permute-start.8 = (bf16[160,128]{1,0:T(8,128)(2,1)S(1)}, bf16[160,128]{1,0:T(8,128)(2,1)S(1)}, u32[]{:S(2)}, u32[]{:S(2)}) collective-permute-start(bf16[160,128]{1,0:T(8,128)(2,1)S(1)} %shard_map.116.now_ref), channel_id=1, source_target_pairs={{0,16},{16,32},{32,48},{48,64},{64,80},{80,96},{96,112},{1,17},{17... | collective-permute-start | bytes 122888 | tf_op jit(solution)/shard_map/ppermute | solution.py:377
  136.5 3.2 %collective-permute-start.9 = (bf16[160,128]{1,0:T(8,128)(2,1)S(1)}, bf16[160,128]{1,0:T(8,128)(2,1)S(1)}, u32[]{:S(2)}, u32[]{:S(2)}) collective-permute-start(bf16[160,128]{1,0:T(8,128)(2,1)S(1)} %shard_map.116.now_ref), channel_id=1, source_target_pairs={{0,32},{16,48},{32,64},{48,80},{64,96},{80,112},{1,33},{17,49},{33... | collective-permute-start | bytes 122888 | tf_op jit(solution)/shard_map/ppermute | solution.py:377
  139.7 0.4 shard_map.117
  140.1 0.0 collective-permute-done.8.one_ref
  140.1 2.2 %collective-permute-done.9.two_ref = bf16[160,128]{1,0:T(8,128)(2,1)S(1)} collective-permute-done((bf16[160,128]{1,0:T(8,128)(2,1)S(1)}, bf16[160,128]{1,0:T(8,128)(2,1)S(1)}, u32[]{:S(2)}, u32[]{:S(2)}) %collective-permute-start.9) | collective-permute-done | bytes 40992 | tf_op jit(solution)/shard_map/ppermute | solution.py:377
  142.4 1.5 %shard_map.118 = bf16[10,64,512]{2,1,0:T(8,128)(2,1)} custom-call(s32[1]{0:T(128)} %bitcast.frame_ref, bf16[160,128]{1,0:T(8,128)(2,1)S(1)} %shard_map.116.now_ref, bf16[160,128]{1,0:T(8,128)(2,1)S(1)} %collective-permute-done.8.one_ref, bf16[160,128]{1,0:T(8,128)(2,1)S(1)} %collective-permute-done.9.two_ref, ...), custom_call_target="tpu_custom_call" | custom-call | tf_op jit(solution)/shard_map/pallas_call | solution.py:359
  (8 shorter events, 0.1 us)
Async XLA Ops:
  0.0 1.3 copy-start
  36.2 8.2 %collective-permute-start.2 = (bf16[2560,128]{1,0:T(8,128)(2,1)S(1)}, bf16[2560,128]{1,0:T(8,128)(2,1)S(1)}, u32[]{:S(2)}, u32[]{:S(2)}) collective-permute-start(bf16[2560,128]{1,0:T(8,128)(2,1)S(1)} %slice.15.refs_0_), channel_id=1, source_target_pairs={{0,1},{1,0},{2,3},{3,2},{4,5},{5,4},{6,7},{7,6},{8,9},{9,8},{10,11... | collective-permute-start | bytes 1966088 | tf_op jit(solution)/shard_map/ppermute | solution.py:372
  36.4 28.5 %collective-permute-start = (bf16[1280,256]{1,0:T(8,128)(2,1)S(1)}, bf16[1280,256]{1,0:T(8,128)(2,1)S(1)}, u32[]{:S(2)}, u32[]{:S(2)}) collective-permute-start(bf16[1280,256]{1,0:T(8,128)(2,1)S(1)} %get-tuple-element.21.refs_1_), channel_id=1, source_target_pairs={{0,32},{32,64},{64,96},{96,0},{1,33},{33,65},{65,97},{97,1},{2,34}... | collective-permute-start | bytes 1966088 | tf_op jit(solution)/shard_map/ppermute | solution.py:372
  38.0 26.9 %collective-permute-start.1 = (bf16[1280,256]{1,0:T(8,128)(2,1)S(1)}, bf16[1280,256]{1,0:T(8,128)(2,1)S(1)}, u32[]{:S(2)}, u32[]{:S(2)}) collective-permute-start(bf16[1280,256]{1,0:T(8,128)(2,1)S(1)} %get-tuple-element.22.refs_2_), channel_id=1, source_target_pairs={{0,96},{32,0},{64,32},{96,64},{1,97},{33,1},{65,33},{97,65},{2,98}... | collective-permute-start | bytes 1966088 | tf_op jit(solution)/shard_map/ppermute | solution.py:372
  44.5 34.4 %collective-permute-start.5 = (bf16[1280,256]{1,0:T(8,128)(2,1)S(1)}, bf16[1280,256]{1,0:T(8,128)(2,1)S(1)}, u32[]{:S(2)}, u32[]{:S(2)}) collective-permute-start(bf16[1280,256]{1,0:T(8,128)(2,1)S(1)} %get-tuple-element.22.refs_2_), channel_id=1, source_target_pairs={{0,32},{32,64},{64,96},{96,0},{1,33},{33,65},{65,97},{97,1},{2,34}... | collective-permute-start | bytes 1966088 | tf_op jit(solution)/shard_map/ppermute | solution.py:372
  58.9 20.0 %collective-permute-start.6 = (bf16[1280,256]{1,0:T(8,128)(2,1)S(1)}, bf16[1280,256]{1,0:T(8,128)(2,1)S(1)}, u32[]{:S(2)}, u32[]{:S(2)}) collective-permute-start(bf16[1280,256]{1,0:T(8,128)(2,1)S(1)} %get-tuple-element.21.refs_1_), channel_id=1, source_target_pairs={{0,96},{32,0},{64,32},{96,64},{1,97},{33,1},{65,33},{97,65},{2,98}... | collective-permute-start | bytes 1966088 | tf_op jit(solution)/shard_map/ppermute | solution.py:372
  64.9 25.5 %collective-permute-start.3 = (bf16[1280,256]{1,0:T(8,128)(2,1)S(1)}, bf16[1280,256]{1,0:T(8,128)(2,1)S(1)}, u32[]{:S(2)}, u32[]{:S(2)}) collective-permute-start(bf16[1280,256]{1,0:T(8,128)(2,1)S(1)} %collective-permute-done.refs_1_), channel_id=1, source_target_pairs={{0,32},{32,64},{64,96},{96,0},{1,33},{33,65},{65,97},{97,1},{2,34}... | collective-permute-start | bytes 1966088 | tf_op jit(solution)/shard_map/ppermute | solution.py:372
  67.0 23.5 %collective-permute-start.4 = (bf16[1280,256]{1,0:T(8,128)(2,1)S(1)}, bf16[1280,256]{1,0:T(8,128)(2,1)S(1)}, u32[]{:S(2)}, u32[]{:S(2)}) collective-permute-start(bf16[1280,256]{1,0:T(8,128)(2,1)S(1)} %collective-permute-done.1.refs_2_), channel_id=1, source_target_pairs={{0,96},{32,0},{64,32},{96,64},{1,97},{33,1},{65,33},{97,65},{2,98}... | collective-permute-start | bytes 1966088 | tf_op jit(solution)/shard_map/ppermute | solution.py:372
  96.3 6.8 %copy-start.1 = (bf16[896,640]{1,0:T(8,128)(2,1)S(1)}, bf16[896,640]{1,0:T(8,128)(2,1)}, u32[]{:S(2)}) copy-start(bf16[896,640]{1,0:T(8,128)(2,1)} %constant.29.clone.choose_ref) | copy-start | bytes 3440644
  96.4 6.8 %collective-permute-start.7 = (f32[144,2560]{1,0:T(8,128)S(1)}, f32[144,2560]{1,0:T(8,128)S(1)}, u32[]{:S(2)}, u32[]{:S(2)}) collective-permute-start(f32[144,2560]{1,0:T(8,128)S(1)} %shard_map.114), channel_id=1, source_target_pairs={{0,1},{1,0},{2,3},{3,2},{4,5},{5,4},{6,7},{7,6},{8,9},{9,8},{10,11... | collective-permute-start | bytes 4423688 | tf_op jit(solution)/shard_map/ppermute | solution.py:372
  105.2 5.3 %copy-start.7 = (bf16[3072,64]{0,1:T(8,128)(2,1)S(1)}, bf16[3072,64]{0,1:T(8,128)(2,1)}, u32[]{:S(2)}) copy-start(bf16[3072,64]{0,1:T(8,128)(2,1)} %param.17) | copy-start | bytes 1179652
  105.2 20.1 %copy-start.2 = (bf16[160,160]{1,0:T(8,128)(2,1)S(1)}, bf16[160,160]{1,0:T(8,128)(2,1)}, u32[]{:S(2)}) copy-start(bf16[160,160]{1,0:T(8,128)(2,1)} %constant.31.clone.order_ref) | copy-start | bytes 153604
  105.2 20.1 %copy-start.3 = (bf16[3,64,128]{2,1,0:T(8,128)(2,1)S(1)}, bf16[3,64,128]{2,1,0:T(8,128)(2,1)}, u32[]{:S(2)}) copy-start(bf16[3,64,128]{2,1,0:T(8,128)(2,1)} %constant.30.clone.choose_ref) | copy-start | bytes 147460
  105.2 20.1 %copy-start.4 = (f32[3072]{0:T(1024)S(1)}, f32[3072]{0:T(1024)}, u32[]{:S(2)}) copy-start(f32[3072]{0:T(1024)} %param.15) | copy-start | bytes 36868
  105.2 20.1 %copy-start.5 = (f32[3072]{0:T(1024)S(1)}, f32[3072]{0:T(1024)}, u32[]{:S(2)}) copy-start(f32[3072]{0:T(1024)} %param.16) | copy-start | bytes 36868
  105.2 20.1 %all-to-all-start.1 = ((bf16[32,112,128]{2,1,0:T(8,128)(2,1)}), bf16[32,112,128]{2,1,0:T(8,128)(2,1)S(1)}, u32[]{:S(2)}, u32[]{:S(2)}) async-start(bf16[32,112,128]{2,1,0:T(8,128)(2,1)} %shard_map.115), calls=%async_computation.1 | async-start | bytes 1835008 | tf_op jit(solution)/shard_map/all_to_all | solution.py:410
  125.4 14.3 %copy-start.6 = (bf16[3,3,3,16,512]{4,3,2,1,0:T(8,128)(2,1)S(1)}, bf16[3,3,3,16,512]{4,3,2,1,0:T(8,128)(2,1)}, u32[]{:S(2)}) copy-start(bf16[3,3,3,16,512]{4,3,2,1,0:T(8,128)(2,1)} %param.18) | copy-start | bytes 1327108
  132.6 7.6 %collective-permute-start.8 = (bf16[160,128]{1,0:T(8,128)(2,1)S(1)}, bf16[160,128]{1,0:T(8,128)(2,1)S(1)}, u32[]{:S(2)}, u32[]{:S(2)}) collective-permute-start(bf16[160,128]{1,0:T(8,128)(2,1)S(1)} %shard_map.116.now_ref), channel_id=1, source_target_pairs={{0,16},{16,32},{32,48},{48,64},{64,80},{80,96},{96,112},{1,17},{17... | collective-permute-start | bytes 122888 | tf_op jit(solution)/shard_map/ppermute | solution.py:377
  136.5 5.9 %collective-permute-start.9 = (bf16[160,128]{1,0:T(8,128)(2,1)S(1)}, bf16[160,128]{1,0:T(8,128)(2,1)S(1)}, u32[]{:S(2)}, u32[]{:S(2)}) collective-permute-start(bf16[160,128]{1,0:T(8,128)(2,1)S(1)} %shard_map.116.now_ref), channel_id=1, source_target_pairs={{0,32},{16,48},{32,64},{48,80},{64,96},{80,112},{1,33},{17,49},{33... | collective-permute-start | bytes 122888 | tf_op jit(solution)/shard_map/ppermute | solution.py:377
